TPU v7x, 1024 devices: a whole 4x8x16 slice. The times are simulated.
1024 devices in a mesh: group: 16 (over y, core), expert: 64 (over z, x).
Axes of the slice: x: 4, y: 8, z: 16, core: 2. Of those that a mesh axis runs over, the one named last changes fastest.
Arguments:
- x_rows: bfloat16 [16, 64, 1, 7168], P('group', 'expert'), may hold values from -6 to 6
- grad_rows: bfloat16 [16, 64, 1, 7168], P('group', 'expert'), may hold values from -6 to 6
- routes: int32 [16, 64, 1, 8], replicated, may hold values from 0 to 63, as said below
- probs: bfloat16 [16, 64, 1, 8], replicated, may hold values from 0.099609375 to 1
- w_gate: bfloat16 [1024, 448, 1024], P(('group', 'expert')), may hold values from -0.0625 to 0.0625
- w_up: bfloat16 [1024, 448, 1024], P(('group', 'expert')), may hold values from -0.0625 to 0.0625
- w_down: bfloat16 [1024, 1024, 448], P(('group', 'expert')), may hold values from -0.1875 to 0.1875
Outputs:
- grad_input: bfloat16 [16, 64, 1, 7168], P('group', 'expert')
Inputs may be any that keep to these rules, and one draw needn't show every extreme that they name: `routes`: each token names 8 different experts from exactly 4 different groups (group of expert j: j // 4), at least one expert in each of them. In each column every group is used by exactly 4 of its 16 tokens, so no expert is named more than 4 times in a column; in every draw some expert is named exactly 4 times in some column.
All inputs are finite; a program needn't handle non-finite values.
Results may differ from a plain program's by a relative error of at most 0.023.
Values may be sent and summed in bfloat16 or wider, within the bound.
A program may use at most 32 MiB of HBM per device.

v0:
```python
import jax
import jax.numpy as jnp
from jax import lax
from jax.sharding import PartitionSpec as P

TOPG = 4
EPG = 4


def from_partner(value, axis, stride):
    mask = 2**stride
    pairs = [(source, source ^ mask) for source in range(lax.axis_size(axis))]
    return lax.ppermute(value, axis, pairs)


def upper_flag(column, bit_level):
    return column // (1 << bit_level) % 2 == 1


def halve(stacked, bit_order, column, partner_swap):
    for bit_level in bit_order:
        half_width = stacked.shape[-1] // 2
        lower_half = stacked[..., :half_width]
        upper_half = stacked[..., half_width:]
        upper_side = upper_flag(column, bit_level)
        outgoing = jnp.where(upper_side, lower_half, upper_half)
        arrived = partner_swap(outgoing, bit_level)
        stacked = jnp.where(upper_side, upper_half, lower_half) + arrived
    return stacked


def regrow(stacked, bit_order, column, partner_swap):
    for bit_level in reversed(bit_order):
        arrived = partner_swap(stacked, bit_level)
        upper_side = upper_flag(column, bit_level)
        stacked = jnp.where(
            upper_side,
            jnp.concatenate([arrived, stacked], axis=-1),
            jnp.concatenate([stacked, arrived], axis=-1),
        )
    return stacked


def on_device(x_rows, grad_rows, routes, probs, w_gate, w_up, w_down):
    groups_count = lax.axis_size("group")
    devices = lax.axis_size("expert")
    my_group = lax.axis_index("group")
    my_column = lax.axis_index("expert")
    pieces = devices // EPG
    levels = pieces.bit_length() - 1
    tokens_here = x_rows.shape[2]
    full_width = x_rows.shape[3]
    piece_width = full_width // pieces
    top_count = routes.shape[3]
    capacity = TOPG * tokens_here
    received_rows = groups_count * tokens_here
    slot_count = devices * capacity
    highest = lax.Precision.HIGHEST
    group_ids = jnp.arange(groups_count, dtype=jnp.int32)
    local_ids = jnp.arange(EPG, dtype=jnp.int32)
    slot_ids = jnp.arange(capacity, dtype=jnp.int32)
    own_routes = lax.dynamic_index_in_dim(
        lax.dynamic_index_in_dim(routes, my_group, 0, keepdims=False), my_column, 0, keepdims=False
    )
    to_group = jnp.any((own_routes // EPG)[None, :, :] == group_ids[:, None, None], axis=2)
    group_mask = to_group.astype(jnp.bfloat16)[:, :, None]
    send_x = group_mask * x_rows[0, 0][None]
    send_g = group_mask * grad_rows[0, 0][None]
    got_x, got_g = (
        lax.all_to_all(send_x, "group", split_axis=0, concat_axis=0, tiled=True),
        lax.all_to_all(send_g, "group", split_axis=0, concat_axis=0, tiled=True),
    )
    column_routes = lax.dynamic_index_in_dim(routes, my_column, 1, keepdims=False)
    wanted = my_group * EPG + local_ids
    held_rows = (
        jnp.any(column_routes[:, :, :, None] == wanted[None, None, None, :], axis=2)
        .astype(jnp.int32)
        .reshape(received_rows, EPG)
    )
    before = jnp.cumsum(held_rows, axis=0) - held_rows
    fan_map = (held_rows.T[:, None, :] == 1) & (before.T[:, None, :] == slot_ids[None, :, None])
    fan_bf = fan_map.astype(jnp.bfloat16)
    out_x = (
        jnp.einsum(
            "ksr,rpd->kpsd",
            fan_bf,
            got_x.reshape(received_rows, pieces, piece_width),
            preferred_element_type=jnp.float32,
        )
        .astype(jnp.bfloat16)
        .reshape(devices, capacity, piece_width)
    )
    out_g = (
        jnp.einsum(
            "ksr,rpd->kpsd",
            fan_bf,
            got_g.reshape(received_rows, pieces, piece_width),
            preferred_element_type=jnp.float32,
        )
        .astype(jnp.bfloat16)
        .reshape(devices, capacity, piece_width)
    )
    slot_x, slot_g = (
        lax.all_to_all(out_x, "expert", split_axis=0, concat_axis=0, tiled=True),
        lax.all_to_all(out_g, "expert", split_axis=0, concat_axis=0, tiled=True),
    )
    rows_x = slot_x.reshape(slot_count, piece_width)
    rows_g = slot_g.reshape(slot_count, piece_width)
    expert_id = my_group * EPG + my_column // pieces
    route_cols = jnp.transpose(routes, (1, 0, 2, 3)).reshape(devices, received_rows, top_count)
    prob_cols = (
        jnp.transpose(probs, (1, 0, 2, 3))
        .reshape(devices, received_rows, top_count)
        .astype(jnp.float32)
    )
    route_hits = route_cols == expert_id
    named_rows = jnp.any(route_hits, axis=2).astype(jnp.int32)
    earlier = jnp.cumsum(named_rows, axis=1) - named_rows
    weight = jnp.sum(prob_cols * route_hits.astype(jnp.float32), axis=2)
    slot_table = (
        (named_rows[:, None, :] == 1) & (earlier[:, None, :] == slot_ids[None, :, None])
    ).astype(jnp.float32)
    row_p = jnp.sum(slot_table * weight[:, None, :], axis=2).reshape(slot_count)
    gate_w = w_gate[0]
    up_w = w_up[0]
    down_w = w_down[0]
    bit_order = list(range(levels - 1, -1, -1))
    gate_part = jnp.dot(rows_x, gate_w, preferred_element_type=jnp.float32)
    up_part = jnp.dot(rows_x, up_w, preferred_element_type=jnp.float32)
    back_part = lax.dot_general(
        rows_g, down_w, (((1,), (1,)), ((), ())), preferred_element_type=jnp.float32
    )
    summed = halve(
        jnp.stack([gate_part, up_part, back_part]),
        bit_order,
        my_column,
        lambda payload, bit_level: from_partner(
            payload.astype(jnp.bfloat16), "expert", bit_level
        ).astype(payload.dtype),
    )
    gate_sum = summed[0]
    up_sum = summed[1]
    back_sum = summed[2]
    back_grad = back_sum * row_p[:, None]
    sigmoid_gate = jax.nn.sigmoid(gate_sum)
    grad_gate = (
        back_grad * up_sum * sigmoid_gate * (1.0 + gate_sum * (1.0 - sigmoid_gate))
    ).astype(jnp.bfloat16)
    grad_up = (back_grad * gate_sum * sigmoid_gate).astype(jnp.bfloat16)
    grown = regrow(
        jnp.stack([grad_gate, grad_up]),
        bit_order,
        my_column,
        lambda payload, bit_level: from_partner(payload, "expert", bit_level),
    )
    slot_grad = lax.dot_general(
        grown[0], gate_w, (((1,), (1,)), ((), ())), preferred_element_type=jnp.float32
    ) + lax.dot_general(
        grown[1], up_w, (((1,), (1,)), ((), ())), preferred_element_type=jnp.float32
    )
    returned = lax.all_to_all(
        slot_grad.reshape(devices, capacity, piece_width).astype(jnp.bfloat16),
        "expert",
        split_axis=0,
        concat_axis=0,
        tiled=True,
    ).astype(jnp.float32)
    regrouped = returned.reshape(EPG, pieces, capacity, piece_width)
    row_grad = jnp.einsum(
        "ksr,kpsd->rpd", fan_map.astype(jnp.float32), regrouped, precision=highest
    ).reshape(groups_count, tokens_here, full_width)
    back_home = lax.all_to_all(
        row_grad.astype(jnp.bfloat16), "group", split_axis=0, concat_axis=0, tiled=True
    ).astype(row_grad.dtype)
    grad_input = jnp.sum(back_home, axis=0).astype(jnp.bfloat16)
    return grad_input[None, None]


def solution(mesh):
    in_specs = (
        P("group", "expert", None, None),
        P("group", "expert", None, None),
        P(),
        P(),
        P(("group", "expert"), None, None),
        P(("group", "expert"), None, None),
        P(("group", "expert"), None, None),
    )
    out_specs = P("group", "expert", None, None)
    return jax.shard_map(
        on_device, mesh=mesh, in_specs=in_specs, out_specs=out_specs, check_vma=False
    )
```

profile of v0, /device:TPU:1, one launch (start us, length us, event | category | flops | bytes accessed | tf_op | source)
XLA Modules:
  0.0 275.3 jit_solution(15231961919255145520)
XLA Ops:
  4.0 2.0 reduce.13
  6.8 17.5 %all-to-all-start = ((bf16[16,2,3584]{2,1,0:T(2,128)(2,1)}), bf16[16,2,3584]{2,1,0:T(2,128)(2,1)S(1)}, u32[]{:S(2)}, u32[]{:S(2)}) async-start(bf16[16,2,3584]{2,1,0:T(2,128)(2,1)} %reshape.326), calls=%async_computation | async-start | bytes 458752 | tf_op jit(solution)/shard_map/all_to_all | solution.py:70
  24.7 2.0 reduce.12
  27.6 7.9 %all-to-all-done = bf16[16,2,3584]{2,1,0:T(2,128)(2,1)S(1)} async-done(((bf16[16,2,3584]{2,1,0:T(2,128)(2,1)}), bf16[16,2,3584]{2,1,0:T(2,128)(2,1)S(1)}, u32[]{:S(2)}, u32[]{:S(2)}) %all-to-all-start) | async-done | bytes 229408 | tf_op jit(solution)/shard_map/all_to_all | solution.py:70
  35.4 3.4 %all-to-all-start.2 = ((bf16[16,2,3584]{2,1,0:T(2,128)(2,1)}), bf16[16,2,3584]{2,1,0:T(2,128)(2,1)S(1)}, u32[]{:S(2)}, u32[]{:S(2)}) async-start(bf16[16,2,3584]{2,1,0:T(2,128)(2,1)} %reshape.324), calls=%async_computation.2 | async-start | bytes 458752 | tf_op jit(solution)/shard_map/all_to_all | solution.py:71
  39.2 1.3 reduce.8
  42.2 6.9 %all-to-all-done.2 = bf16[16,2,3584]{2,1,0:T(2,128)(2,1)S(1)} async-done(((bf16[16,2,3584]{2,1,0:T(2,128)(2,1)}), bf16[16,2,3584]{2,1,0:T(2,128)(2,1)S(1)}, u32[]{:S(2)}, u32[]{:S(2)}) %all-to-all-start.2) | async-done | bytes 229408 | tf_op jit(solution)/shard_map/all_to_all | solution.py:71
  49.1 13.2 %all-to-all-start.1 = ((bf16[64,4,448]{2,1,0:T(4,128)(2,1)}), bf16[64,4,448]{2,1,0:T(4,128)(2,1)S(1)}, u32[]{:S(2)}, u32[]{:S(2)}) async-start(bf16[64,4,448]{2,1,0:T(4,128)(2,1)} %copy.63), calls=%async_computation.1 | async-start | bytes 524288 | tf_op jit(solution)/shard_map/all_to_all | solution.py:104
  65.5 17.4 %all-to-all-done.1 = bf16[64,4,448]{2,1,0:T(4,128)(2,1)S(1)} async-done(((bf16[64,4,448]{2,1,0:T(4,128)(2,1)}), bf16[64,4,448]{2,1,0:T(4,128)(2,1)S(1)}, u32[]{:S(2)}, u32[]{:S(2)}) %all-to-all-start.1) | async-done | bytes 229408 | tf_op jit(solution)/shard_map/all_to_all | solution.py:104
  83.0 6.3 %all-to-all-start.3 = ((bf16[64,4,448]{2,1,0:T(4,128)(2,1)}), bf16[64,4,448]{2,1,0:T(4,128)(2,1)S(1)}, u32[]{:S(2)}, u32[]{:S(2)}) async-start(bf16[64,4,448]{2,1,0:T(4,128)(2,1)} %copy.68), calls=%async_computation.3 | async-start | bytes 524288 | tf_op jit(solution)/shard_map/all_to_all | solution.py:105
  90.6 17.2 %all-to-all-done.3 = bf16[64,4,448]{2,1,0:T(4,128)(2,1)S(1)} async-done(((bf16[64,4,448]{2,1,0:T(4,128)(2,1)}), bf16[64,4,448]{2,1,0:T(4,128)(2,1)S(1)}, u32[]{:S(2)}, u32[]{:S(2)}) %all-to-all-start.3) | async-done | bytes 229408 | tf_op jit(solution)/shard_map/all_to_all | solution.py:105
  107.9 1.7 convolution_bitcast_fusion.1
  109.9 1.7 copy-done.1
  111.7 1.9 collective-permute-start
  113.7 36.5 %collective-permute-done = bf16[3,256,512]{1,2,0:T(8,128)(2,1)S(1)} collective-permute-done((bf16[3,256,512]{1,2,0:T(8,128)(2,1)S(1)}, bf16[3,256,512]{1,2,0:T(8,128)(2,1)S(1)}, u32[]{:S(2)}, u32[]{:S(2)}) %collective-permute-start) | collective-permute-done | bytes 786464 | tf_op jit(solution)/shard_map/ppermute | solution.py:13
  150.2 2.1 convert_add_fusion
  152.4 1.9 collective-permute-start.1
  154.7 9.2 %collective-permute-done.1 = bf16[3,256,256]{1,2,0:T(8,128)(2,1)} collective-permute-done((bf16[3,256,256]{1,2,0:T(8,128)(2,1)S(1)}, bf16[3,256,256]{1,2,0:T(8,128)(2,1)}, u32[]{:S(2)}, u32[]{:S(2)}) %collective-permute-start.1) | collective-permute-done | bytes 393248 | tf_op jit(solution)/shard_map/ppermute | solution.py:13
  165.0 4.5 %collective-permute-start.2 = (bf16[3,256,128]{1,2,0:T(8,128)(2,1)S(1)}, bf16[3,256,128]{1,2,0:T(8,128)(2,1)S(1)}, u32[]{:S(2)}, u32[]{:S(2)}) collective-permute-start(bf16[3,256,128]{1,2,0:T(8,128)(2,1)S(1)} %select_convert_fusion.2), channel_id=1, source_target_pairs={{0,2},{1,3},{2,0},{3,1},{4,6},{5,7},{6,4},{7,5},{8,10},{9,11},{10,... | collective-permute-start | bytes 589832 | tf_op jit(solution)/shard_map/ppermute | solution.py:13
  169.8 3.2 %collective-permute-done.2 = bf16[3,256,128]{1,2,0:T(8,128)(2,1)S(1)} collective-permute-done((bf16[3,256,128]{1,2,0:T(8,128)(2,1)S(1)}, bf16[3,256,128]{1,2,0:T(8,128)(2,1)S(1)}, u32[]{:S(2)}, u32[]{:S(2)}) %collective-permute-start.2) | collective-permute-done | bytes 196640 | tf_op jit(solution)/shard_map/ppermute | solution.py:13
  173.1 3.2 %collective-permute-start.3 = (bf16[3,256,64]{1,2,0:T(8,128)(2,1)S(1)}, bf16[3,256,64]{1,2,0:T(8,128)(2,1)S(1)}, u32[]{:S(2)}, u32[]{:S(2)}) collective-permute-start(bf16[3,256,64]{1,2,0:T(8,128)(2,1)S(1)} %select_convert_fusion.3), channel_id=1, source_target_pairs={{0,1},{1,0},{2,3},{3,2},{4,5},{5,4},{6,7},{7,6},{8,9},{9,8},{10,11... | collective-permute-start | bytes 294920 | tf_op jit(solution)/shard_map/ppermute | solution.py:13
  176.4 2.0 collective-permute-done.3
  178.5 3.2 %collective-permute-start.4 = (bf16[2,256,64]{1,2,0:T(8,128)(2,1)S(1)}, bf16[2,256,64]{1,2,0:T(8,128)(2,1)S(1)}, u32[]{:S(2)}, u32[]{:S(2)}) collective-permute-start(bf16[2,256,64]{1,2,0:T(8,128)(2,1)S(1)} %pad_maximum_fusion.1), channel_id=1, source_target_pairs={{0,1},{1,0},{2,3},{3,2},{4,5},{5,4},{6,7},{7,6},{8,9},{9,8},{10,11... | collective-permute-start | bytes 196616 | tf_op jit(solution)/shard_map/ppermute | solution.py:13
  181.7 1.9 collective-permute-done.4
  183.6 4.5 %collective-permute-start.5 = (bf16[2,256,128]{1,2,0:T(8,128)(2,1)S(1)}, bf16[2,256,128]{1,2,0:T(8,128)(2,1)S(1)}, u32[]{:S(2)}, u32[]{:S(2)}) collective-permute-start(bf16[2,256,128]{1,2,0:T(8,128)(2,1)S(1)} %maximum_select_fusion.3), channel_id=1, source_target_pairs={{0,2},{1,3},{2,0},{3,1},{4,6},{5,7},{6,4},{7,5},{8,10},{9,11},{10,... | collective-permute-start | bytes 393224 | tf_op jit(solution)/shard_map/ppermute | solution.py:13
  188.1 3.4 %collective-permute-done.5 = bf16[2,256,128]{1,2,0:T(8,128)(2,1)S(1)} collective-permute-done((bf16[2,256,128]{1,2,0:T(8,128)(2,1)S(1)}, bf16[2,256,128]{1,2,0:T(8,128)(2,1)S(1)}, u32[]{:S(2)}, u32[]{:S(2)}) %collective-permute-start.5) | collective-permute-done | bytes 131104 | tf_op jit(solution)/shard_map/ppermute | solution.py:13
  191.6 2.1 collective-permute-start.6
  193.7 5.0 %collective-permute-done.6 = bf16[2,256,256]{1,2,0:T(8,128)(2,1)S(1)} collective-permute-done((bf16[2,256,256]{1,2,0:T(8,128)(2,1)S(1)}, bf16[2,256,256]{1,2,0:T(8,128)(2,1)S(1)}, u32[]{:S(2)}, u32[]{:S(2)}) %collective-permute-start.6) | collective-permute-done | bytes 262176 | tf_op jit(solution)/shard_map/ppermute | solution.py:13
  198.9 3.8 %collective-permute-start.7 = (bf16[2,256,512]{1,2,0:T(8,128)(2,1)S(1)}, bf16[2,256,512]{1,2,0:T(8,128)(2,1)S(1)}, u32[]{:S(2)}, u32[]{:S(2)}) collective-permute-start(bf16[2,256,512]{1,2,0:T(8,128)(2,1)S(1)} %maximum_select_fusion.1), channel_id=1, source_target_pairs={{0,8},{1,9},{2,10},{3,11},{4,12},{5,13},{6,14},{7,15},{8,0},{9,1},... | collective-permute-start | bytes 1572872 | tf_op jit(solution)/shard_map/ppermute | solution.py:13
  202.8 22.2 %collective-permute-done.7 = bf16[2,256,512]{1,2,0:T(8,128)(2,1)S(1)} collective-permute-done((bf16[2,256,512]{1,2,0:T(8,128)(2,1)S(1)}, bf16[2,256,512]{1,2,0:T(8,128)(2,1)S(1)}, u32[]{:S(2)}, u32[]{:S(2)}) %collective-permute-start.7) | collective-permute-done | bytes 524320 | tf_op jit(solution)/shard_map/ppermute | solution.py:13
  226.4 26.3 %all_to_all.30 = bf16[64,4,448]{2,1,0:T(4,128)(2,1)S(1)} all-to-all(bf16[64,4,448]{2,1,0:T(4,128)(2,1)S(1)} %convert_element_type.122), channel_id=1, replica_groups=mesh['group'=16,'expert'=64] {'expert'}, dimensions={0} | all-to-all | bytes 458752 | tf_op jit(solution)/shard_map/all_to_all | solution.py:161
  254.3 19.7 %all_to_all.31 = bf16[16,2,3584]{2,1,0:T(2,128)(2,1)S(1)} all-to-all(bf16[16,2,3584]{2,1,0:T(2,128)(2,1)S(1)} %reshape.328), channel_id=1, replica_groups=mesh['group'=16,'expert'=64] {'group'}, dimensions={0} | all-to-all | bytes 458752 | tf_op jit(solution)/shard_map/all_to_all | solution.py:172
  (85 shorter events, 19.7 us)
Async XLA Ops:
  0.0 90.0 %copy-start = (bf16[1,448,1024]{2,1,0:T(8,128)(2,1)S(1)}, bf16[1,448,1024]{2,1,0:T(8,128)(2,1)}, u32[]{:S(2)}) copy-start(bf16[1,448,1024]{2,1,0:T(8,128)(2,1)} %param.11) | copy-start | bytes 2752516
  0.0 24.3 %copy-start.4 = (s32[16,64,1,8]{1,3,2,0:T(8,128)S(1)}, s32[16,64,1,8]{1,3,2,0:T(8,128)}, u32[]{:S(2)}) copy-start(s32[16,64,1,8]{1,3,2,0:T(8,128)} %param.9) | copy-start | bytes 98308
  6.8 28.6 %all-to-all-start = ((bf16[16,2,3584]{2,1,0:T(2,128)(2,1)}), bf16[16,2,3584]{2,1,0:T(2,128)(2,1)S(1)}, u32[]{:S(2)}, u32[]{:S(2)}) async-start(bf16[16,2,3584]{2,1,0:T(2,128)(2,1)} %reshape.326), calls=%async_computation | async-start | bytes 458752 | tf_op jit(solution)/shard_map/all_to_all | solution.py:70
  35.4 13.7 %all-to-all-start.2 = ((bf16[16,2,3584]{2,1,0:T(2,128)(2,1)}), bf16[16,2,3584]{2,1,0:T(2,128)(2,1)S(1)}, u32[]{:S(2)}, u32[]{:S(2)}) async-start(bf16[16,2,3584]{2,1,0:T(2,128)(2,1)} %reshape.324), calls=%async_computation.2 | async-start | bytes 458752 | tf_op jit(solution)/shard_map/all_to_all | solution.py:71
  49.1 33.8 %all-to-all-start.1 = ((bf16[64,4,448]{2,1,0:T(4,128)(2,1)}), bf16[64,4,448]{2,1,0:T(4,128)(2,1)S(1)}, u32[]{:S(2)}, u32[]{:S(2)}) async-start(bf16[64,4,448]{2,1,0:T(4,128)(2,1)} %copy.63), calls=%async_computation.1 | async-start | bytes 524288 | tf_op jit(solution)/shard_map/all_to_all | solution.py:104
  62.5 27.0 %copy-start.2 = (bf16[1,448,1024]{2,1,0:T(8,128)(2,1)S(1)}, bf16[1,448,1024]{2,1,0:T(8,128)(2,1)}, u32[]{:S(2)}) copy-start(bf16[1,448,1024]{2,1,0:T(8,128)(2,1)} %param.12) | copy-start | bytes 2752516
  83.0 24.9 %all-to-all-start.3 = ((bf16[64,4,448]{2,1,0:T(4,128)(2,1)}), bf16[64,4,448]{2,1,0:T(4,128)(2,1)S(1)}, u32[]{:S(2)}, u32[]{:S(2)}) async-start(bf16[64,4,448]{2,1,0:T(4,128)(2,1)} %copy.68), calls=%async_computation.3 | async-start | bytes 524288 | tf_op jit(solution)/shard_map/all_to_all | solution.py:105
  109.9 1.7 copy-start.1
  111.7 38.5 %collective-permute-start = (bf16[3,256,512]{1,2,0:T(8,128)(2,1)S(1)}, bf16[3,256,512]{1,2,0:T(8,128)(2,1)S(1)}, u32[]{:S(2)}, u32[]{:S(2)}) collective-permute-start(bf16[3,256,512]{1,2,0:T(8,128)(2,1)S(1)} %select_convert_fusion), channel_id=1, source_target_pairs={{0,8},{1,9},{2,10},{3,11},{4,12},{5,13},{6,14},{7,15},{8,0},{9,1},... | collective-permute-start | bytes 2359304 | tf_op jit(solution)/shard_map/ppermute | solution.py:13
  113.7 40.6 %copy-start.5 = (s32[16,64,1,8]{1,3,2,0:T(8,128)S(1)}, s32[16,64,1,8]{1,3,2,0:T(8,128)}, u32[]{:S(2)}) copy-start(s32[16,64,1,8]{1,3,2,0:T(8,128)} %param.9) | copy-start | bytes 98308
  152.4 17.3 %copy-start.6 = (bf16[16,64,1,8]{1,3,2,0:T(8,128)(2,1)S(1)}, bf16[16,64,1,8]{1,3,2,0:T(8,128)(2,1)}, u32[]{:S(2)}) copy-start(bf16[16,64,1,8]{1,3,2,0:T(8,128)(2,1)} %param.10) | copy-start | bytes 49156
  152.4 11.5 %collective-permute-start.1 = (bf16[3,256,256]{1,2,0:T(8,128)(2,1)S(1)}, bf16[3,256,256]{1,2,0:T(8,128)(2,1)}, u32[]{:S(2)}, u32[]{:S(2)}) collective-permute-start(bf16[3,256,256]{1,2,0:T(8,128)(2,1)S(1)} %select_convert_fusion.1), channel_id=1, source_target_pairs={{0,4},{1,5},{2,6},{3,7},{4,0},{5,1},{6,2},{7,3},{8,12},{9,13},{10,... | collective-permute-start | bytes 1179656 | tf_op jit(solution)/shard_map/ppermute | solution.py:13
  165.0 7.9 %collective-permute-start.2 = (bf16[3,256,128]{1,2,0:T(8,128)(2,1)S(1)}, bf16[3,256,128]{1,2,0:T(8,128)(2,1)S(1)}, u32[]{:S(2)}, u32[]{:S(2)}) collective-permute-start(bf16[3,256,128]{1,2,0:T(8,128)(2,1)S(1)} %select_convert_fusion.2), channel_id=1, source_target_pairs={{0,2},{1,3},{2,0},{3,1},{4,6},{5,7},{6,4},{7,5},{8,10},{9,11},{10,... | collective-permute-start | bytes 589832 | tf_op jit(solution)/shard_map/ppermute | solution.py:13
  173.1 5.4 %collective-permute-start.3 = (bf16[3,256,64]{1,2,0:T(8,128)(2,1)S(1)}, bf16[3,256,64]{1,2,0:T(8,128)(2,1)S(1)}, u32[]{:S(2)}, u32[]{:S(2)}) collective-permute-start(bf16[3,256,64]{1,2,0:T(8,128)(2,1)S(1)} %select_convert_fusion.3), channel_id=1, source_target_pairs={{0,1},{1,0},{2,3},{3,2},{4,5},{5,4},{6,7},{7,6},{8,9},{9,8},{10,11... | collective-permute-start | bytes 294920 | tf_op jit(solution)/shard_map/ppermute | solution.py:13
  178.5 5.0 %collective-permute-start.4 = (bf16[2,256,64]{1,2,0:T(8,128)(2,1)S(1)}, bf16[2,256,64]{1,2,0:T(8,128)(2,1)S(1)}, u32[]{:S(2)}, u32[]{:S(2)}) collective-permute-start(bf16[2,256,64]{1,2,0:T(8,128)(2,1)S(1)} %pad_maximum_fusion.1), channel_id=1, source_target_pairs={{0,1},{1,0},{2,3},{3,2},{4,5},{5,4},{6,7},{7,6},{8,9},{9,8},{10,11... | collective-permute-start | bytes 196616 | tf_op jit(solution)/shard_map/ppermute | solution.py:13
  183.6 7.9 %collective-permute-start.5 = (bf16[2,256,128]{1,2,0:T(8,128)(2,1)S(1)}, bf16[2,256,128]{1,2,0:T(8,128)(2,1)S(1)}, u32[]{:S(2)}, u32[]{:S(2)}) collective-permute-start(bf16[2,256,128]{1,2,0:T(8,128)(2,1)S(1)} %maximum_select_fusion.3), channel_id=1, source_target_pairs={{0,2},{1,3},{2,0},{3,1},{4,6},{5,7},{6,4},{7,5},{8,10},{9,11},{10,... | collective-permute-start | bytes 393224 | tf_op jit(solution)/shard_map/ppermute | solution.py:13
  191.6 7.1 %collective-permute-start.6 = (bf16[2,256,256]{1,2,0:T(8,128)(2,1)S(1)}, bf16[2,256,256]{1,2,0:T(8,128)(2,1)S(1)}, u32[]{:S(2)}, u32[]{:S(2)}) collective-permute-start(bf16[2,256,256]{1,2,0:T(8,128)(2,1)S(1)} %maximum_select_fusion.2), channel_id=1, source_target_pairs={{0,4},{1,5},{2,6},{3,7},{4,0},{5,1},{6,2},{7,3},{8,12},{9,13},{10,... | collective-permute-start | bytes 786440 | tf_op jit(solution)/shard_map/ppermute | solution.py:13
  198.9 26.8 %copy-start.3 = (bf16[1,448,1024]{2,1,0:T(8,128)(2,1)S(1)}, bf16[1,448,1024]{2,1,0:T(8,128)(2,1)}, u32[]{:S(2)}) copy-start(bf16[1,448,1024]{2,1,0:T(8,128)(2,1)} %param.12) | copy-start | bytes 2752516
  198.9 26.1 %collective-permute-start.7 = (bf16[2,256,512]{1,2,0:T(8,128)(2,1)S(1)}, bf16[2,256,512]{1,2,0:T(8,128)(2,1)S(1)}, u32[]{:S(2)}, u32[]{:S(2)}) collective-permute-start(bf16[2,256,512]{1,2,0:T(8,128)(2,1)S(1)} %maximum_select_fusion.1), channel_id=1, source_target_pairs={{0,8},{1,9},{2,10},{3,11},{4,12},{5,13},{6,14},{7,15},{8,0},{9,1},... | collective-permute-start | bytes 1572872 | tf_op jit(solution)/shard_map/ppermute | solution.py:13
where the time goes:
time: 276 us; the launch traced here: 275 us
  waiting for transfers between devices  133 us (48%)
  starting transfers between devices  65.4 us (24%)
  blocking collectives  46 us (17%)
  other arithmetic  15.3 us (6%)
  local copies, waits for them, and re-layouts  10.7 us (4%)
  matrix products  4.59 us (2%)
    ppermute x8, waiting for transfers between devices, from_partner(): return lax.ppermute(value, axis, pairs)  83.3 us
    all_to_all x1, blocking collectives, on_device(): lax.all_to_all(slot_grad.reshape(devices, capacity, piece_width).astype(j...  26.3 us
    ppermute x8, starting transfers between devices, from_partner(): return lax.ppermute(value, axis, pairs)  25.1 us
    all_to_all x1, blocking collectives, on_device(): lax.all_to_all(row_grad.astype(jnp.bfloat16), 'group', split_axis=0, conc...  19.7 us
    all_to_all x1, starting transfers between devices, on_device(): lax.all_to_all(send_x, 'group', split_axis=0, concat_axis=0, tiled=True)  17.5 us
    all_to_all x1, waiting for transfers between devices, on_device(): lax.all_to_all(out_x, 'expert', split_axis=0, concat_axis=0, tiled=True)  17.4 us
    all_to_all x1, waiting for transfers between devices, on_device(): lax.all_to_all(out_g, 'expert', split_axis=0, concat_axis=0, tiled=True)  17.2 us
    all_to_all x1, starting transfers between devices, on_device(): lax.all_to_all(out_x, 'expert', split_axis=0, concat_axis=0, tiled=True)  13.2 us
  transfers between devices with their start and end apart: 12, of which 12 were waited for; matrix products, arithmetic and copies ran while one was open for 4% of the time, Pallas kernels for 0%

commit v1 on v0

v1 whole, which is shorter than its diff:
```python
import functools

import jax
import jax.numpy as jnp
from jax import lax
from jax.experimental import pallas as pl
from jax.experimental.pallas import tpu as pltpu
from jax.sharding import PartitionSpec as P

MESH = pl.DeviceIdType.MESH
BLOCKS = 4
RANKS = 4
RING = 4
SLOTS = 4


def low(value, size):
    return value & (size - 1)


def high(value, size):
    return value >> (size.bit_length() - 1)


def onehot(mask):
    return jnp.where(mask, 1.0, 0.0).astype(jnp.bfloat16)


def exact_dot(left, right):
    return jnp.dot(left, right, preferred_element_type=jnp.float32)


def dot_nt(left, right):
    return lax.dot_general(left, right, (((1,), (1,)), ((), ())), preferred_element_type=jnp.float32)


def kernel(
    sizes,
    slot_ref,
    tok_ref,
    rowp_ref,
    wg_hbm,
    wu_hbm,
    wd_hbm,
    out_ref,
    wg,
    wu,
    wd,
    got_a,
    sel,
    got_x,
    blk,
    rows,
    part,
    got_rx,
    part_z,
    got_rz,
    grads,
    ret,
    got_ret,
    ret_x,
    got_retx,
    scat,
    fin,
    w_sem,
    a_send,
    a_recv,
    x_send,
    x_recv,
    z_send,
    z_recv,
    rx_send,
    rx_recv,
    rz_send,
    rz_recv,
    gz_send,
    gz_recv,
    gx_send,
    gx_recv,
    tz_send,
    tz_recv,
    tx_send,
    tx_recv,
    tg_send,
    tg_recv,
):
    groups, blocks, ranks, ring, slots = sizes
    depth = blocks * ranks
    pieces = ranks * ring
    chunk = ring * slots
    width = tok_ref.shape[2]
    hidden = wg.shape[1]
    my_g = lax.axis_index("group")
    my_e = lax.axis_index("expert")
    my_x = low(my_e, ring)
    my_z = high(my_e, ring)
    my_r = low(my_z, ranks)
    z_base = my_z - my_r

    def at_x(x):
        return (my_g, my_z * ring + x)

    def at_z(z):
        return (my_g, z * ring + my_x)

    def at_g(g):
        return (g, my_e)

    def remote(src, dst, send, recv, device):
        return pltpu.make_async_remote_copy(
            src_ref=src, dst_ref=dst, send_sem=send, recv_sem=recv, device_id=device, device_id_type=MESH
        )

    sent = []

    def go(copy):
        copy.start()
        sent.append(copy)

    weight_copies = [
        pltpu.make_async_copy(source, target, w_sem.at[at])
        for at, (source, target) in enumerate(((wg_hbm, wg), (wu_hbm, wu), (wd_hbm, wd)))
    ]
    for copy in weight_copies:
        copy.start()

    barrier = pltpu.get_barrier_semaphore()
    for d in range(1, groups):
        pl.semaphore_signal(barrier, inc=1, device_id=at_g(low(my_g + d, groups)), device_id_type=MESH)
    for d in range(1, depth):
        pl.semaphore_signal(barrier, inc=1, device_id=at_z(low(my_z + d, depth)), device_id_type=MESH)
    for d in range(1, ring):
        pl.semaphore_signal(barrier, inc=1, device_id=at_x(low(my_x + d, ring)), device_id_type=MESH)
    pl.semaphore_wait(barrier, groups + depth + ring - 3)

    def spread(a):
        for d in range(1, groups):
            go(remote(tok_ref.at[a], got_a.at[a, my_g], a_send.at[a, d], a_recv.at[a, d], at_g(low(my_g + d, groups))))
        got_a[a, my_g] = tok_ref[a]

    spread(0)
    slot_rows = ring * ranks * slots
    token_rows = groups * pieces

    def slot_of(index):
        s = low(index, slots)
        token = jnp.full(index.shape, slot_ref[0], jnp.int32)
        for at in range(1, slots):
            token = jnp.where(s == at, slot_ref[at], token)
        rest = high(index, slots)
        piece = low(rest, ranks) * ring + high(rest, ranks)
        return token * pieces + piece

    shape = (slot_rows, token_rows)
    pick = onehot(
        slot_of(lax.broadcasted_iota(jnp.int32, shape, 0)) == lax.broadcasted_iota(jnp.int32, shape, 1)
    )
    shape = (token_rows, slot_rows)
    unpick = onehot(
        slot_of(lax.broadcasted_iota(jnp.int32, shape, 1)) == lax.broadcasted_iota(jnp.int32, shape, 0)
    )
    shape = (slot_rows, slot_rows)
    row = lax.broadcasted_iota(jnp.int32, shape, 0)
    rest = high(row, slots)
    turned = (low(rest, ring) * ranks + high(rest, ring)) * slots + low(row, slots)
    turn = onehot(lax.broadcasted_iota(jnp.int32, shape, 1) == turned)
    shape = (slot_rows, blocks * slot_rows)
    row = lax.broadcasted_iota(jnp.int32, shape, 0)
    rest = high(row, slots)
    turned = (low(rest, ranks) * ring + high(rest, ranks)) * slots + low(row, slots)
    fold = onehot(low(lax.broadcasted_iota(jnp.int32, shape, 1), slot_rows) == turned)

    def gather_tokens(a):
        for d in range(1, groups):
            slot = got_a.at[a, low(my_g - d, groups)]
            remote(slot, slot, a_send.at[a, d], a_recv.at[a, d], at_g(my_g)).wait_recv()

    def cross(a):
        chosen = exact_dot(pick, got_a[a].reshape(token_rows, width)).astype(jnp.bfloat16)
        sel[a] = chosen.reshape(ring, ranks * slots, width)
        for d in range(1, ring):
            to = low(my_x + d, ring)
            go(remote(sel.at[a, to], got_x.at[a, my_x], x_send.at[a, d], x_recv.at[a, d], at_x(to)))
        got_x[a, my_x] = sel[a, my_x]
        for d in range(1, ring):
            slot = got_x.at[a, low(my_x - d, ring)]
            remote(slot, slot, x_send.at[a, d], x_recv.at[a, d], at_x(my_x)).wait_recv()
        mixed = exact_dot(turn, got_x[a].reshape(slot_rows, width)).astype(jnp.bfloat16)
        blk[a] = mixed.reshape(ranks, chunk, width)

    def send_deep(a):
        for d in range(1, depth):
            to = low(my_z + d, depth)
            go(remote(blk.at[a, low(to, ranks)], rows.at[a, my_z], z_send.at[a, d], z_recv.at[a, d], at_z(to)))
        rows[a, my_z] = blk[a, my_r]

    def wait_deep(a):
        for d in range(1, depth):
            slot = rows.at[a, low(my_z - d, depth)]
            remote(slot, slot, z_send.at[a, d], z_recv.at[a, d], at_z(my_z)).wait_recv()

    def ring_send(q, value):
        part[q] = value.astype(jnp.bfloat16).reshape(ring, ranks * chunk, hidden)
        for d in range(1, ring):
            to = low(my_x + d, ring)
            go(remote(part.at[q, to], got_rx.at[q, d], rx_send.at[q, d], rx_recv.at[q, d], at_x(to)))

    def line_send(q):
        total = part[q, my_x].astype(jnp.float32)
        for d in range(1, ring):
            slot = got_rx.at[q, d]
            remote(slot, slot, rx_send.at[q, d], rx_recv.at[q, d], at_x(my_x)).wait_recv()
            total += got_rx[q, d].astype(jnp.float32)
        part_z[q] = total.astype(jnp.bfloat16).reshape(ranks, chunk, hidden)
        for d in range(1, ranks):
            to = low(my_r + d, ranks)
            go(remote(part_z.at[q, to], got_rz.at[q, d], rz_send.at[q, d], rz_recv.at[q, d], at_z(z_base + to)))

    def line_sum(q):
        total = part_z[q, my_r].astype(jnp.float32)
        for d in range(1, ranks):
            slot = got_rz.at[q, d]
            remote(slot, slot, rz_send.at[q, d], rz_recv.at[q, d], at_z(my_z)).wait_recv()
            total += got_rz[q, d].astype(jnp.float32)
        return total

    gather_tokens(0)
    spread(1)
    cross(0)
    send_deep(0)
    gather_tokens(1)
    cross(1)
    wait_deep(0)
    send_deep(1)
    rows_x = rows[0].reshape(depth * chunk, width)
    weight_copies[0].wait()
    ring_send(0, exact_dot(rows_x, wg[...]))
    weight_copies[1].wait()
    ring_send(1, exact_dot(rows_x, wu[...]))
    wait_deep(1)
    weight_copies[2].wait()
    ring_send(2, dot_nt(rows[1].reshape(depth * chunk, width), wd[...]))
    line_send(0)
    line_send(1)
    line_send(2)
    gate = line_sum(0)
    up = line_sum(1)
    back = line_sum(2) * rowp_ref[...]
    sig = 1.0 / (1.0 + jnp.exp(-gate))
    mine = my_x * ranks + my_r
    grads[mine, 0] = (back * up * sig * (1.0 + gate * (1.0 - sig))).astype(jnp.bfloat16)
    grads[mine, 1] = (back * gate * sig).astype(jnp.bfloat16)

    for d in range(1, ranks):
        to = z_base + low(my_r + d, ranks)
        go(remote(grads.at[mine], grads.at[mine], gz_send.at[d], gz_recv.at[d], at_z(to)))
    for d in range(1, ranks):
        slot = grads.at[my_x * ranks + low(my_r - d, ranks)]
        remote(slot, slot, gz_send.at[d], gz_recv.at[d], at_z(my_z)).wait_recv()
    held = grads.at[pl.ds(my_x * ranks, ranks)]
    for d in range(1, ring):
        go(remote(held, held, gx_send.at[d], gx_recv.at[d], at_x(low(my_x + d, ring))))

    for d in (0, 1, 3, 2) if ring == 4 else range(ring):
        owner = low(my_x - d, ring)
        first = owner * ranks
        if d:
            slot = grads.at[pl.ds(first, ranks)]
            remote(slot, slot, gx_send.at[d], gx_recv.at[d], at_x(my_x)).wait_recv()
        both = grads[pl.ds(first, ranks)]
        result = dot_nt(both[:, 0].reshape(ranks * chunk, hidden), wg[...])
        result += dot_nt(both[:, 1].reshape(ranks * chunk, hidden), wu[...])
        ret[pl.ds(first, ranks)] = result.astype(jnp.bfloat16).reshape(ranks, chunk, width)
        for j in range(ranks):
            to = first + j

            @pl.when(to != my_z)
            def _():
                remote(ret.at[to], got_ret.at[my_z], tz_send.at[to], tz_recv.at[my_z], at_z(to)).start()

    got_ret[my_z] = ret[my_z]
    for d in range(1, depth):
        source = low(my_z - d, depth)
        slot = got_ret.at[source]
        remote(slot, slot, tz_send.at[source], tz_recv.at[source], at_z(my_z)).wait_recv()
    folded = exact_dot(fold, got_ret[...].reshape(blocks * slot_rows, width)).astype(jnp.bfloat16)
    ret_x[...] = folded.reshape(ring, ranks * slots, width)
    for d in range(1, ring):
        to = low(my_x + d, ring)
        go(remote(ret_x.at[to], got_retx.at[my_x], tx_send.at[d], tx_recv.at[d], at_x(to)))
    got_retx[my_x] = ret_x[my_x]
    for d in range(1, ring):
        slot = got_retx.at[low(my_x - d, ring)]
        remote(slot, slot, tx_send.at[d], tx_recv.at[d], at_x(my_x)).wait_recv()
    spread_rows = exact_dot(unpick, got_retx[...].reshape(slot_rows, width)).astype(jnp.bfloat16)
    scat[...] = spread_rows.reshape(groups, pieces, width)
    for d in range(1, groups):
        to = low(my_g + d, groups)
        go(remote(scat.at[to], fin.at[d], tg_send.at[d], tg_recv.at[d], at_g(to)))
    total = scat[my_g].astype(jnp.float32)
    for d in range(1, groups):
        slot = fin.at[d]
        remote(slot, slot, tg_send.at[d], tg_recv.at[d], at_g(my_g)).wait_recv()
        total += fin[d].astype(jnp.float32)
    out_ref[...] = total.astype(jnp.bfloat16)

    for copy in sent:
        copy.wait_send()
    for d in range(1, depth):
        to = low(my_z + d, depth)
        remote(ret.at[to], got_ret.at[my_z], tz_send.at[to], tz_recv.at[my_z], at_z(to)).wait_send()


def run(sizes, slot_tokens, tokens, row_p, w_gate, w_up, w_down):
    groups, blocks, ranks, ring, slots = sizes
    depth, pieces, chunk = blocks * ranks, ranks * ring, ring * slots
    width, hidden = w_gate.shape
    bf = jnp.bfloat16
    vmem = functools.partial(pltpu.VMEM, dtype=bf)
    dma = pltpu.SemaphoreType.DMA
    any_spec = pl.BlockSpec(memory_space=pl.ANY)
    vmem_spec = pl.BlockSpec(memory_space=pltpu.VMEM)
    return pl.pallas_call(
        functools.partial(kernel, sizes),
        out_shape=jax.ShapeDtypeStruct((pieces, width), bf),
        in_specs=[pl.BlockSpec(memory_space=pltpu.SMEM), vmem_spec, vmem_spec, any_spec, any_spec, any_spec],
        out_specs=vmem_spec,
        scratch_shapes=[
            vmem((width, hidden)),
            vmem((width, hidden)),
            vmem((hidden, width)),
            vmem((2, groups, pieces, width)),
            vmem((2, ring, ranks * slots, width)),
            vmem((2, ring, ranks * slots, width)),
            vmem((2, ranks, chunk, width)),
            vmem((2, depth, chunk, width)),
            vmem((3, ring, ranks * chunk, hidden)),
            vmem((3, ring, ranks * chunk, hidden)),
            vmem((3, ranks, chunk, hidden)),
            vmem((3, ranks, chunk, hidden)),
            vmem((depth, 2, chunk, hidden)),
            vmem((depth, chunk, width)),
            vmem((depth, chunk, width)),
            vmem((ring, ranks * slots, width)),
            vmem((ring, ranks * slots, width)),
            vmem((groups, pieces, width)),
            vmem((groups, pieces, width)),
            dma((3,)),
            dma((2, groups)),
            dma((2, groups)),
            dma((2, ring)),
            dma((2, ring)),
            dma((2, depth)),
            dma((2, depth)),
            dma((3, ring)),
            dma((3, ring)),
            dma((3, ranks)),
            dma((3, ranks)),
            dma((ranks,)),
            dma((ranks,)),
            dma((ring,)),
            dma((ring,)),
            dma((depth,)),
            dma((depth,)),
            dma((ring,)),
            dma((ring,)),
            dma((groups,)),
            dma((groups,)),
        ],
        compiler_params=pltpu.CompilerParams(
            collective_id=0, has_side_effects=True, vmem_limit_bytes=40 * 1024 * 1024
        ),
    )(slot_tokens, tokens, row_p, w_gate, w_up, w_down)


def slot_maps(named):
    tokens = named.shape[0]
    order = jnp.arange(tokens, dtype=jnp.int32)
    ahead = (order[:, None] > order[None, :]).astype(jnp.int32)
    before = jnp.sum(
        ahead.reshape((tokens, tokens) + (1,) * (named.ndim - 1)) * named[None].astype(jnp.int32), axis=1
    )
    return named[..., None] & (before[..., None] == jnp.arange(SLOTS, dtype=jnp.int32))


def on_device(x_rows, grad_rows, routes, probs, w_gate, w_up, w_down, sizes):
    groups, blocks, ranks, ring, slots = sizes
    my_g = lax.axis_index("group")
    my_e = lax.axis_index("expert")
    my_z, my_x = my_e // ring, my_e % ring
    width = w_gate.shape[1]
    pieces = ranks * ring
    tokens = jnp.stack([x_rows.reshape(pieces, width), grad_rows.reshape(pieces, width)])
    column = lax.dynamic_slice_in_dim(routes, my_e, 1, 1)[:, 0, 0]
    mask = slot_maps(jnp.any(column // blocks == my_g, axis=1))
    slot_tokens = jnp.sum(mask * jnp.arange(groups, dtype=jnp.int32)[:, None], axis=0)
    owned = (my_x * ranks + my_z % ranks) * ring
    near = lax.dynamic_slice_in_dim(routes, owned, ring, 1)[:, :, 0]
    near_p = lax.dynamic_slice_in_dim(probs, owned, ring, 1)[:, :, 0].astype(jnp.float32)
    expert = my_g * blocks + my_z // ranks
    mask = slot_maps(jnp.any(near // blocks == my_g, axis=2))
    weight = jnp.sum(jnp.where(near == expert, near_p, 0.0), axis=2)
    row_p = jnp.sum(jnp.where(mask, weight[:, :, None], 0.0), axis=0).reshape(ring * slots, 1)
    result = run(sizes, slot_tokens, tokens, row_p, w_gate[0], w_up[0], w_down[0])
    return result.reshape(x_rows.shape)


def solution(mesh):
    sizes = (mesh.shape["group"], BLOCKS, RANKS, RING, SLOTS)
    in_specs = (
        P("group", "expert", None, None),
        P("group", "expert", None, None),
        P(),
        P(),
        P(("group", "expert"), None, None),
        P(("group", "expert"), None, None),
        P(("group", "expert"), None, None),
    )
    return jax.shard_map(
        functools.partial(on_device, sizes=sizes),
        mesh=mesh,
        in_specs=in_specs,
        out_specs=P("group", "expert", None, None),
        check_vma=False,
    )
```

time: 276 us -> 129 us (0.47)
  waiting for transfers between devices: 133 us -> 0 us
  Pallas kernels: 0 us -> 123 us
  starting transfers between devices: 65.4 us -> 0 us
  blocking collectives: 46 us -> 0 us
  other arithmetic: 15.3 us -> 0.94 us
  local copies, waits for them, and re-layouts: 10.7 us -> 5.33 us
  matrix products: 4.59 us -> 0 us
    pallas_call x0 -> x1, Pallas kernels: none -> 123 us  [run(): pl.pallas_call(functools.partial(kernel, sizes), out_shape=jax.ShapeDtype...]
    ppermute x8 -> x0, waiting for transfers between devices: 83.3 us -> none  [from_partner(): return lax.ppermute(value, axis, pairs)]
    all_to_all x4 -> x0, waiting for transfers between devices: 49.4 us -> none  [the longest x1 17.4 us: on_device(): lax.all_to_all(out_x, 'expert', split_axis=0, concat_axis=0, tiled=True)]
    all_to_all x2 -> x0, blocking collectives: 46 us -> none  [the longest x1 26.3 us: on_device(): lax.all_to_all(slot_grad.reshape(devices, capacity, piece_width).astype(j...]
    all_to_all x4 -> x0, starting transfers between devices: 40.4 us -> none  [the longest x1 17.5 us: on_device(): lax.all_to_all(send_x, 'group', split_axis=0, concat_axis=0, tiled=True)]
    ppermute x8 -> x0, starting transfers between devices: 25.1 us -> none  [from_partner(): return lax.ppermute(value, axis, pairs)]
    mul x3 -> x0, other arithmetic: 4.68 us -> none  [on_device(): send_x = group_mask * x_rows[0, 0][None]]
    dot_general x8 -> x0, matrix products: 4.59 us -> none  [the longest x1 1.74 us: on_device(): lax.dot_general(rows_g, down_w, (((1,), (1,)), ((), ())), preferred_eleme...]
  transfers between devices with their start and end apart: 12 -> 0, of which waited for: 12 -> 0; matrix products, arithmetic and copies ran while one was open for 4% -> 0% of each run, Pallas kernels for 0% -> 0%
where the time goes in v1:
time: 129 us
  Pallas kernels  123 us (95%)
  local copies, waits for them, and re-layouts  5.33 us (4%)
    pallas_call x1, Pallas kernels, run(): pl.pallas_call(functools.partial(kernel, sizes), out_shape=jax.ShapeDtype...  123 us
    unnamed x14, local copies, waits for them, and re-layouts  4.09 us

profile of v1, /device:TPU:1, one launch (start us, length us, event | category | flops | bytes accessed | tf_op | source)
XLA Modules:
  0.0 129.1 jit_solution(9203638116679270055)
XLA Ops:
  0.0 0.0 copy-start.2
  0.0 0.8 copy-done.2
  0.8 0.0 copy-start.3
  0.8 0.1 fusion.5
  1.0 0.1 copy.21
  1.1 0.5 copy-done.3
  1.6 0.1 fusion.2
  1.7 0.0 copy-start.4
  1.7 0.1 copy.23
  1.8 0.1 multiply_reduce_fusion
  2.0 0.1 select_reduce_fusion
  2.1 0.1 reshape.38.rowp_ref
  2.1 0.3 copy-done.4
  2.5 0.0 copy-start.5
  2.5 0.1 reduce
  2.6 0.1 stack_reshape.6
  2.6 0.6 copy-done.5
  3.2 0.1 reduce.1
  3.3 0.1 stack_reshape.7
  3.4 0.1 constant_dynamic-slice_fusion
  3.5 0.1 copy.26
  3.7 0.1 select_reduce_fusion.1
  3.8 0.1 select_reduce_fusion.2.slot_ref
  3.9 0.0 copy-start
  3.9 0.0 copy-start.1
  3.9 1.6 %copy.24 = bf16[1,1024,448]{2,1,0:T(8,128)(2,1)S(1)} copy(bf16[1,1024,448]{1,2,0:T(8,128)(2,1)} %param.13) | data formatting | bytes 1835008 | tf_op args[6]
  5.5 0.0 copy-done
  5.5 0.1 copy-done.1
  5.6 122.7 %shard_map.73 = bf16[16,448]{1,0:T(8,128)(2,1)S(1)} custom-call(s32[4]{0:T(128)S(1)} %select_reduce_fusion.2.slot_ref, bf16[2,16,448]{2,1,0:T(8,128)(2,1)S(1)} %pad_maximum_fusion.tok_ref, f32[16,1]{1,0:T(8,128)S(1)} %reshape.38.rowp_ref, bf16[448,1024]{1,0:T(8,128)(2,1)S(1)} %bitcast.46, bf16[448,1024]{1,0:T(8,128)(2,1)S(1)} %bitcast.47, ...), custom_call_target="tpu_custom_call" | custom-call | tf_op jit(solution)/shard_map/pallas_call | solution.py:323
  128.3 0.7 reshape.36
  (5 shorter events, 0.1 us)
Async XLA Ops:
  0.0 0.8 copy-start.2
  0.8 0.8 copy-start.3
  1.7 0.8 copy-start.4
  2.5 0.7 copy-start.5
  3.9 1.6 %copy-start = (bf16[1,448,1024]{2,1,0:T(8,128)(2,1)S(1)}, bf16[1,448,1024]{2,1,0:T(8,128)(2,1)}, u32[]{:S(2)}) copy-start(bf16[1,448,1024]{2,1,0:T(8,128)(2,1)} %param.11) | copy-start | bytes 2752516
  3.9 1.7 %copy-start.1 = (bf16[1,448,1024]{2,1,0:T(8,128)(2,1)S(1)}, bf16[1,448,1024]{2,1,0:T(8,128)(2,1)}, u32[]{:S(2)}) copy-start(bf16[1,448,1024]{2,1,0:T(8,128)(2,1)} %param.12) | copy-start | bytes 2752516

commit v2 on v1

--- a/solution.py
+++ b/solution.py
@@ -36,9 +36,9 @@
 
 def kernel(
     sizes,
-    slot_ref,
     tok_ref,
-    rowp_ref,
+    route_ref,
+    prob_ref,
     wg_hbm,
     wu_hbm,
     wd_hbm,
@@ -46,11 +46,17 @@
     wg,
     wu,
     wd,
+    pair,
     got_a,
+    got_b,
     sel,
+    sel_b,
     got_x,
+    got_xb,
     blk,
+    blk_b,
     rows,
+    rows_b,
     part,
     got_rx,
     part_z,
@@ -63,8 +69,12 @@
     scat,
     fin,
     w_sem,
+    p_send,
+    p_recv,
     a_send,
     a_recv,
+    c_send,
+    c_recv,
     x_send,
     x_recv,
     z_send,
@@ -88,6 +98,8 @@
     depth = blocks * ranks
     pieces = ranks * ring
     chunk = ring * slots
+    lines = groups // 2
+    half = depth // 2
     width = tok_ref.shape[2]
     hidden = wg.shape[1]
     my_g = lax.axis_index("group")
@@ -96,6 +108,15 @@
     my_z = high(my_e, ring)
     my_r = low(my_z, ranks)
     z_base = my_z - my_r
+    my_core = low(my_g, 2)
+    my_y = high(my_g, 2)
+    my_half = high(my_z, half)
+
+    def chunk_of(z):
+        return low(z, half) * 2 + high(z, half)
+
+    def z_of(at):
+        return low(at, 2) * half + high(at, 2)
 
     def at_x(x):
         return (my_g, my_z * ring + x)
@@ -111,6 +132,7 @@
             src_ref=src, dst_ref=dst, send_sem=send, recv_sem=recv, device_id=device, device_id_type=MESH
         )
 
+    around = sorted(range(1, ring), key=lambda d: min(d, ring - d))
     sent = []
 
     def go(copy):
@@ -131,34 +153,65 @@
         pl.semaphore_signal(barrier, inc=1, device_id=at_z(low(my_z + d, depth)), device_id_type=MESH)
     for d in range(1, ring):
         pl.semaphore_signal(barrier, inc=1, device_id=at_x(low(my_x + d, ring)), device_id_type=MESH)
-    pl.semaphore_wait(barrier, groups + depth + ring - 3)
-
-    def spread(a):
-        for d in range(1, groups):
-            go(remote(tok_ref.at[a], got_a.at[a, my_g], a_send.at[a, d], a_recv.at[a, d], at_g(low(my_g + d, groups))))
-        got_a[a, my_g] = tok_ref[a]
-
-    spread(0)
+
     slot_rows = ring * ranks * slots
     token_rows = groups * pieces
 
-    def slot_of(index):
+    route = route_ref[...]
+    columns = route.shape[2]
+    in_group = jnp.max(jnp.where(high(route, blocks) == my_g, 1.0, 0.0), axis=1)
+    expert = my_g * blocks + high(my_z, ranks)
+    weight = jnp.sum(jnp.where(route == expert, prob_ref[...].astype(jnp.float32), 0.0), axis=1)
+    lane = lax.broadcasted_iota(jnp.int32, (1, columns), 1)
+    count = jnp.zeros((1, columns), jnp.float32)
+    slot_token = [count] * slots
+    slot_weight = [count] * slots
+    for m in range(groups):
+        named = in_group[m : m + 1]
+        for s in range(slots):
+            here = jnp.where(count == s, named, 0.0)
+            slot_token[s] += here * (m % 2 * lines + m // 2)
+            slot_weight[s] += here * weight[m : m + 1]
+        count += named
+
+    def tokens_of(column):
+        return [
+            jnp.sum(jnp.where(lane == column, token, 0.0), axis=1, keepdims=True).astype(jnp.int32)
+            for token in slot_token
+        ]
+
+    my_tokens = tokens_of(my_e)
+    pair_tokens = [tokens_of((h * half + low(my_z, half)) * ring + my_x) for h in range(2)]
+    row = lax.broadcasted_iota(jnp.int32, (chunk, columns), 0)
+    owned = z_of(my_x * ranks + my_r) * ring
+    row_p = jnp.zeros((chunk, columns), jnp.float32)
+    for s in range(slots):
+        row_p = jnp.where(low(row, slots) == s, slot_weight[s], row_p)
+    owner = owned + high(row, slots) == lax.broadcasted_iota(jnp.int32, (chunk, columns), 1)
+    row_p = jnp.sum(jnp.where(owner, row_p, 0.0), axis=1, keepdims=True)
+
+    def slot_of(index, tokens):
         s = low(index, slots)
-        token = jnp.full(index.shape, slot_ref[0], jnp.int32)
+        token = jnp.broadcast_to(tokens[0], index.shape)
         for at in range(1, slots):
-            token = jnp.where(s == at, slot_ref[at], token)
+            token = jnp.where(s == at, tokens[at], token)
         rest = high(index, slots)
         piece = low(rest, ranks) * ring + high(rest, ranks)
         return token * pieces + piece
 
-    shape = (slot_rows, token_rows)
-    pick = onehot(
-        slot_of(lax.broadcasted_iota(jnp.int32, shape, 0)) == lax.broadcasted_iota(jnp.int32, shape, 1)
-    )
+    def picking(tokens):
+        shape = (slot_rows, token_rows)
+        return onehot(
+            slot_of(lax.broadcasted_iota(jnp.int32, shape, 0), tokens)
+            == lax.broadcasted_iota(jnp.int32, shape, 1)
+        )
+
     shape = (token_rows, slot_rows)
     unpick = onehot(
-        slot_of(lax.broadcasted_iota(jnp.int32, shape, 1)) == lax.broadcasted_iota(jnp.int32, shape, 0)
+        slot_of(lax.broadcasted_iota(jnp.int32, shape, 1), my_tokens)
+        == lax.broadcasted_iota(jnp.int32, shape, 0)
     )
+    picks = [picking(my_tokens)] + [picking(tokens) for tokens in pair_tokens]
     shape = (slot_rows, slot_rows)
     row = lax.broadcasted_iota(jnp.int32, shape, 0)
     rest = high(row, slots)
@@ -170,38 +223,58 @@
     turned = (low(rest, ranks) * ring + high(rest, ranks)) * slots + low(row, slots)
     fold = onehot(low(lax.broadcasted_iota(jnp.int32, shape, 1), slot_rows) == turned)
 
-    def gather_tokens(a):
-        for d in range(1, groups):
-            slot = got_a.at[a, low(my_g - d, groups)]
+    pl.semaphore_wait(barrier, groups + depth + ring - 3)
+
+    far_first = sorted(range(1, lines), key=lambda d: -min(d, lines - d))
+
+    def spread(a, source, target):
+        for d in far_first:
+            to = low(my_y + d, lines) * 2 + my_core
+            go(remote(source, target.at[my_core, my_y], a_send.at[a, d], a_recv.at[a, d], at_g(to)))
+        target[my_core, my_y] = source[...]
+
+    def share(a, target):
+        for d in range(1, lines):
+            slot = target.at[my_core, low(my_y - d, lines)]
             remote(slot, slot, a_send.at[a, d], a_recv.at[a, d], at_g(my_g)).wait_recv()
-
-    def cross(a):
-        chosen = exact_dot(pick, got_a[a].reshape(token_rows, width)).astype(jnp.bfloat16)
-        sel[a] = chosen.reshape(ring, ranks * slots, width)
+        mine = target.at[my_core]
+        go(remote(mine, mine, c_send.at[a], c_recv.at[a], at_g(my_y * 2 + 1 - my_core)))
+
+    def wait_share(a, target):
+        slot = target.at[1 - my_core]
+        remote(slot, slot, c_send.at[a], c_recv.at[a], at_g(my_g)).wait_recv()
+
+    def ring_swap(a, source, target):
         for d in range(1, ring):
             to = low(my_x + d, ring)
-            go(remote(sel.at[a, to], got_x.at[a, my_x], x_send.at[a, d], x_recv.at[a, d], at_x(to)))
-        got_x[a, my_x] = sel[a, my_x]
+            go(remote(source.at[to], target.at[my_x], x_send.at[a, d], x_recv.at[a, d], at_x(to)))
+        target[my_x] = source[my_x]
+
+    def wait_swap(a, target):
         for d in range(1, ring):
-            slot = got_x.at[a, low(my_x - d, ring)]
+            slot = target.at[low(my_x - d, ring)]
             remote(slot, slot, x_send.at[a, d], x_recv.at[a, d], at_x(my_x)).wait_recv()
-        mixed = exact_dot(turn, got_x[a].reshape(slot_rows, width)).astype(jnp.bfloat16)
-        blk[a] = mixed.reshape(ranks, chunk, width)
-
-    def send_deep(a):
-        for d in range(1, depth):
-            to = low(my_z + d, depth)
-            go(remote(blk.at[a, low(to, ranks)], rows.at[a, my_z], z_send.at[a, d], z_recv.at[a, d], at_z(to)))
-        rows[a, my_z] = blk[a, my_r]
-
-    def wait_deep(a):
-        for d in range(1, depth):
-            slot = rows.at[a, low(my_z - d, depth)]
+
+    near = list(range(1, depth // 4 + 1)) + list(range(depth - depth // 4 + 1, depth))
+    near.sort(key=lambda d: min(d, depth - d))
+    all_z = sorted(range(1, depth), key=lambda d: min(d, depth - d))
+
+    way = 1 - 2 * my_core
+
+    def send_deep(a, steps, source, slot):
+        for d in steps:
+            to = low(my_z + way * d, depth)
+            go(remote(source.at[low(to, ranks)], slot, z_send.at[a, d], z_recv.at[a, d], at_z(to)))
+        slot[...] = source[my_r]
+
+    def wait_deep(a, steps, slot_from):
+        for d in steps:
+            slot = slot_from(low(my_z - way * d, depth))
             remote(slot, slot, z_send.at[a, d], z_recv.at[a, d], at_z(my_z)).wait_recv()
 
     def ring_send(q, value):
         part[q] = value.astype(jnp.bfloat16).reshape(ring, ranks * chunk, hidden)
-        for d in range(1, ring):
+        for d in around:
             to = low(my_x + d, ring)
             go(remote(part.at[q, to], got_rx.at[q, d], rx_send.at[q, d], rx_recv.at[q, d], at_x(to)))
 
@@ -224,28 +297,47 @@
             total += got_rz[q, d].astype(jnp.float32)
         return total
 
-    gather_tokens(0)
-    spread(1)
-    cross(0)
-    send_deep(0)
-    gather_tokens(1)
-    cross(1)
-    wait_deep(0)
-    send_deep(1)
-    rows_x = rows[0].reshape(depth * chunk, width)
+    spread(0, tok_ref.at[0], got_a)
+    go(remote(tok_ref.at[1], pair.at[my_half], p_send, p_recv, at_z(low(my_z + half, depth))))
+    pair[my_half] = tok_ref[1]
+    share(0, got_a)
+    slot = pair.at[1 - my_half]
+    remote(slot, slot, p_send, p_recv, at_z(my_z)).wait_recv()
+    spread(1, pair, got_b)
+    wait_share(0, got_a)
+    chosen = exact_dot(picks[0], got_a[...].reshape(token_rows, width)).astype(jnp.bfloat16)
+    sel[...] = chosen.reshape(ring, ranks * slots, width)
+    ring_swap(0, sel, got_x)
+    wait_swap(0, got_x)
+    mixed = exact_dot(turn, got_x[...].reshape(slot_rows, width)).astype(jnp.bfloat16)
+    blk[...] = mixed.reshape(ranks, chunk, width)
+    send_deep(0, all_z, blk, rows.at[chunk_of(my_z)])
+    share(1, got_b)
+    wait_share(1, got_b)
+    for h in range(2):
+        chosen = exact_dot(picks[1 + h], got_b[:, :, h].reshape(token_rows, width)).astype(jnp.bfloat16)
+        sel_b[:, h] = chosen.reshape(ring, ranks * slots, width)
+    ring_swap(1, sel_b, got_xb)
+    wait_swap(1, got_xb)
+    for h in range(2):
+        mixed = exact_dot(turn, got_xb[:, h].reshape(slot_rows, width)).astype(jnp.bfloat16)
+        blk_b[:, h] = mixed.reshape(ranks, chunk, width)
+    send_deep(1, near, blk_b, rows_b.at[low(my_z, half)])
+    wait_deep(0, all_z, lambda z: rows.at[chunk_of(z)])
+    rows_x = rows[...].reshape(depth * chunk, width)
     weight_copies[0].wait()
     ring_send(0, exact_dot(rows_x, wg[...]))
     weight_copies[1].wait()
     ring_send(1, exact_dot(rows_x, wu[...]))
-    wait_deep(1)
+    wait_deep(1, near, lambda z: rows_b.at[low(z, half)])
     weight_copies[2].wait()
-    ring_send(2, dot_nt(rows[1].reshape(depth * chunk, width), wd[...]))
+    ring_send(2, exact_dot(rows_b[...].reshape(depth * chunk, width), wd[...]))
     line_send(0)
     line_send(1)
     line_send(2)
     gate = line_sum(0)
     up = line_sum(1)
-    back = line_sum(2) * rowp_ref[...]
+    back = line_sum(2) * row_p
     sig = 1.0 / (1.0 + jnp.exp(-gate))
     mine = my_x * ranks + my_r
     grads[mine, 0] = (back * up * sig * (1.0 + gate * (1.0 - sig))).astype(jnp.bfloat16)
@@ -258,10 +350,10 @@
         slot = grads.at[my_x * ranks + low(my_r - d, ranks)]
         remote(slot, slot, gz_send.at[d], gz_recv.at[d], at_z(my_z)).wait_recv()
     held = grads.at[pl.ds(my_x * ranks, ranks)]
-    for d in range(1, ring):
+    for d in around:
         go(remote(held, held, gx_send.at[d], gx_recv.at[d], at_x(low(my_x + d, ring))))
 
-    for d in (0, 1, 3, 2) if ring == 4 else range(ring):
+    for d in [0] + around:
         owner = low(my_x - d, ring)
         first = owner * ranks
         if d:
@@ -272,13 +364,14 @@
         result += dot_nt(both[:, 1].reshape(ranks * chunk, hidden), wu[...])
         ret[pl.ds(first, ranks)] = result.astype(jnp.bfloat16).reshape(ranks, chunk, width)
         for j in range(ranks):
-            to = first + j
+            at = first + j
+            to = z_of(at)
 
             @pl.when(to != my_z)
-            def _():
-                remote(ret.at[to], got_ret.at[my_z], tz_send.at[to], tz_recv.at[my_z], at_z(to)).start()
-
-    got_ret[my_z] = ret[my_z]
+            def _(at=at, to=to):
+                remote(ret.at[at], got_ret.at[my_z], tz_send.at[to], tz_recv.at[my_z], at_z(to)).start()
+
+    got_ret[my_z] = ret[chunk_of(my_z)]
     for d in range(1, depth):
         source = low(my_z - d, depth)
         slot = got_ret.at[source]
@@ -296,8 +389,8 @@
     scat[...] = spread_rows.reshape(groups, pieces, width)
     for d in range(1, groups):
         to = low(my_g + d, groups)
-        go(remote(scat.at[to], fin.at[d], tg_send.at[d], tg_recv.at[d], at_g(to)))
-    total = scat[my_g].astype(jnp.float32)
+        go(remote(scat.at[low(to, 2) * lines + high(to, 2)], fin.at[d], tg_send.at[d], tg_recv.at[d], at_g(to)))
+    total = scat[low(my_g, 2) * lines + high(my_g, 2)].astype(jnp.float32)
     for d in range(1, groups):
         slot = fin.at[d]
         remote(slot, slot, tg_send.at[d], tg_recv.at[d], at_g(my_g)).wait_recv()
@@ -308,10 +401,10 @@
         copy.wait_send()
     for d in range(1, depth):
         to = low(my_z + d, depth)
-        remote(ret.at[to], got_ret.at[my_z], tz_send.at[to], tz_recv.at[my_z], at_z(to)).wait_send()
-
-
-def run(sizes, slot_tokens, tokens, row_p, w_gate, w_up, w_down):
+        remote(ret.at[chunk_of(to)], got_ret.at[my_z], tz_send.at[to], tz_recv.at[my_z], at_z(to)).wait_send()
+
+
+def run(sizes, tokens, routes, probs, w_gate, w_up, w_down):
     groups, blocks, ranks, ring, slots = sizes
     depth, pieces, chunk = blocks * ranks, ranks * ring, ring * slots
     width, hidden = w_gate.shape
@@ -323,17 +416,23 @@
     return pl.pallas_call(
         functools.partial(kernel, sizes),
         out_shape=jax.ShapeDtypeStruct((pieces, width), bf),
-        in_specs=[pl.BlockSpec(memory_space=pltpu.SMEM), vmem_spec, vmem_spec, any_spec, any_spec, any_spec],
+        in_specs=[vmem_spec, vmem_spec, vmem_spec, any_spec, any_spec, any_spec],
         out_specs=vmem_spec,
         scratch_shapes=[
             vmem((width, hidden)),
             vmem((width, hidden)),
-            vmem((hidden, width)),
-            vmem((2, groups, pieces, width)),
-            vmem((2, ring, ranks * slots, width)),
-            vmem((2, ring, ranks * slots, width)),
-            vmem((2, ranks, chunk, width)),
-            vmem((2, depth, chunk, width)),
+            vmem((width, hidden)),
+            vmem((2, pieces, width)),
+            vmem((2, groups // 2, pieces, width)),
+            vmem((2, groups // 2, 2, pieces, width)),
+            vmem((ring, ranks * slots, width)),
+            vmem((ring, 2, ranks * slots, width)),
+            vmem((ring, ranks * slots, width)),
+            vmem((ring, 2, ranks * slots, width)),
+            vmem((ranks, chunk, width)),
+            vmem((ranks, 2, chunk, width)),
+            vmem((depth, chunk, width)),
+            vmem((depth // 2, 2, chunk, width)),
             vmem((3, ring, ranks * chunk, hidden)),
             vmem((3, ring, ranks * chunk, hidden)),
             vmem((3, ranks, chunk, hidden)),
@@ -346,8 +445,12 @@
             vmem((groups, pieces, width)),
             vmem((groups, pieces, width)),
             dma((3,)),
-            dma((2, groups)),
-            dma((2, groups)),
+            dma(()),
+            dma(()),
+            dma((2, groups // 2)),
+            dma((2, groups // 2)),
+            dma((2,)),
+            dma((2,)),
             dma((2, ring)),
             dma((2, ring)),
             dma((2, depth)),
@@ -370,38 +473,15 @@
         compiler_params=pltpu.CompilerParams(
             collective_id=0, has_side_effects=True, vmem_limit_bytes=40 * 1024 * 1024
         ),
-    )(slot_tokens, tokens, row_p, w_gate, w_up, w_down)
-
-
-def slot_maps(named):
-    tokens = named.shape[0]
-    order = jnp.arange(tokens, dtype=jnp.int32)
-    ahead = (order[:, None] > order[None, :]).astype(jnp.int32)
-    before = jnp.sum(
-        ahead.reshape((tokens, tokens) + (1,) * (named.ndim - 1)) * named[None].astype(jnp.int32), axis=1
-    )
-    return named[..., None] & (before[..., None] == jnp.arange(SLOTS, dtype=jnp.int32))
+    )(tokens, routes, probs, w_gate, w_up, w_down)
 
 
 def on_device(x_rows, grad_rows, routes, probs, w_gate, w_up, w_down, sizes):
     groups, blocks, ranks, ring, slots = sizes
-    my_g = lax.axis_index("group")
-    my_e = lax.axis_index("expert")
-    my_z, my_x = my_e // ring, my_e % ring
-    width = w_gate.shape[1]
-    pieces = ranks * ring
+    pieces, width = ranks * ring, w_gate.shape[1]
     tokens = jnp.stack([x_rows.reshape(pieces, width), grad_rows.reshape(pieces, width)])
-    column = lax.dynamic_slice_in_dim(routes, my_e, 1, 1)[:, 0, 0]
-    mask = slot_maps(jnp.any(column // blocks == my_g, axis=1))
-    slot_tokens = jnp.sum(mask * jnp.arange(groups, dtype=jnp.int32)[:, None], axis=0)
-    owned = (my_x * ranks + my_z % ranks) * ring
-    near = lax.dynamic_slice_in_dim(routes, owned, ring, 1)[:, :, 0]
-    near_p = lax.dynamic_slice_in_dim(probs, owned, ring, 1)[:, :, 0].astype(jnp.float32)
-    expert = my_g * blocks + my_z // ranks
-    mask = slot_maps(jnp.any(near // blocks == my_g, axis=2))
-    weight = jnp.sum(jnp.where(near == expert, near_p, 0.0), axis=2)
-    row_p = jnp.sum(jnp.where(mask, weight[:, :, None], 0.0), axis=0).reshape(ring * slots, 1)
-    result = run(sizes, slot_tokens, tokens, row_p, w_gate[0], w_up[0], w_down[0])
+    by_column = [jnp.swapaxes(array[:, :, 0], 1, 2) for array in (routes, probs)]
+    result = run(sizes, tokens, *by_column, w_gate[0], w_up[0], jnp.swapaxes(w_down[0], 0, 1))
     return result.reshape(x_rows.shape)
 
 

time: 129 us -> 123 us (0.953)
  Pallas kernels: 123 us -> 117 us
    pallas_call x1, Pallas kernels: 123 us -> 117 us  [run(): pl.pallas_call(functools.partial(kernel, sizes), out_shape=jax.ShapeDtype...]
    unnamed x14 -> x12, local copies, waits for them, and re-layouts: 4.09 us -> 4.29 us
where the time goes in v2:
time: 123 us
  Pallas kernels  117 us (95%)
  local copies, waits for them, and re-layouts  5.18 us (4%)
    pallas_call x1, Pallas kernels, run(): pl.pallas_call(functools.partial(kernel, sizes), out_shape=jax.ShapeDtype...  117 us
    unnamed x12, local copies, waits for them, and re-layouts  4.29 us

profile of v2, /device:TPU:1, one launch (start us, length us, event | category | flops | bytes accessed | tf_op | source)
XLA Modules:
  0.0 123.0 jit_solution(12078466711018876415)
XLA Ops:
  0.0 0.0 copy-start.5
  0.0 0.8 reduce
  0.8 0.1 stack_reshape.6
  0.9 0.0 copy-done.5
  0.9 0.0 copy-start.3
  1.0 0.1 reduce.1
  1.0 0.1 stack_reshape.7
  1.1 0.0 copy-start.4
  1.1 0.6 copy-done.3
  1.8 0.1 copy-done.4
  1.9 0.0 copy-start
  1.9 1.2 copy-done
  3.1 0.0 copy-start.1
  3.1 1.2 copy-done.1
  4.3 0.0 copy-start.2
  4.3 1.2 copy-done.2
  5.4 116.8 %shard_map.73 = bf16[16,448]{1,0:T(8,128)(2,1)S(1)} custom-call(bf16[2,16,448]{2,1,0:T(8,128)(2,1)S(1)} %pad_maximum_fusion.tok_ref, s32[16,8,64]{2,1,0:T(8,128)S(1)} %bitcast.14, bf16[16,8,64]{2,1,0:T(8,128)(2,1)S(1)} %bitcast.15, bf16[448,1024]{1,0:T(8,128)(2,1)S(1)} %bitcast.11, bf16[448,1024]{1,0:T(8,128)(2,1)S(1)} %bitcast.12, ...), custom_call_target="tpu_custom_call" | custom-call | tf_op jit(solution)/shard_map/pallas_call | solution.py:416
  122.3 0.7 reshape.3
  (1 shorter events, 0.0 us)
Async XLA Ops:
  0.0 0.9 copy-start.5
  0.9 0.8 copy-start.3
  1.1 0.8 copy-start.4
  1.9 1.2 copy-start
  3.1 1.2 copy-start.1
  4.3 1.2 copy-start.2

commit v3 on v2

--- a/solution.py
+++ b/solution.py
@@ -37,12 +37,14 @@
 def kernel(
     sizes,
     tok_ref,
-    route_ref,
-    prob_ref,
+    route_hbm,
+    prob_hbm,
     wg_hbm,
     wu_hbm,
     wd_hbm,
     out_ref,
+    route_ref,
+    prob_ref,
     wg,
     wu,
     wd,
@@ -61,6 +63,10 @@
     got_rx,
     part_z,
     got_rz,
+    part_zb,
+    got_zb,
+    part_xb,
+    got_rxb,
     grads,
     ret,
     got_ret,
@@ -69,6 +75,7 @@
     scat,
     fin,
     w_sem,
+    m_sem,
     p_send,
     p_recv,
     a_send,
@@ -83,6 +90,10 @@
     rx_recv,
     rz_send,
     rz_recv,
+    bz_send,
+    bz_recv,
+    bx_send,
+    bx_recv,
     gz_send,
     gz_recv,
     gx_send,
@@ -139,6 +150,12 @@
         copy.start()
         sent.append(copy)
 
+    map_copies = [
+        pltpu.make_async_copy(source, target, m_sem.at[at])
+        for at, (source, target) in enumerate(((route_hbm, route_ref), (prob_hbm, prob_ref)))
+    ]
+    for copy in map_copies:
+        copy.start()
     weight_copies = [
         pltpu.make_async_copy(source, target, w_sem.at[at])
         for at, (source, target) in enumerate(((wg_hbm, wg), (wu_hbm, wu), (wd_hbm, wd)))
@@ -157,6 +174,8 @@
     slot_rows = ring * ranks * slots
     token_rows = groups * pieces
 
+    for copy in map_copies:
+        copy.wait()
     route = route_ref[...]
     columns = route.shape[2]
     in_group = jnp.max(jnp.where(high(route, blocks) == my_g, 1.0, 0.0), axis=1)
@@ -331,34 +350,53 @@
     ring_send(1, exact_dot(rows_x, wu[...]))
     wait_deep(1, near, lambda z: rows_b.at[low(z, half)])
     weight_copies[2].wait()
-    ring_send(2, exact_dot(rows_b[...].reshape(depth * chunk, width), wd[...]))
+    back_part = exact_dot(rows_b[...].reshape(depth * chunk, width), wd[...])
+    back_part = back_part.astype(jnp.bfloat16).reshape(ring, ranks, chunk, hidden)
+    for r in range(ranks):
+        part_zb[r] = back_part[:, r]
+    for d in range(1, ranks):
+        to = my_r ^ d
+        go(remote(part_zb.at[to], got_zb.at[d], bz_send.at[d], bz_recv.at[d], at_z(z_base + to)))
     line_send(0)
     line_send(1)
-    line_send(2)
+    total = part_zb[my_r].astype(jnp.float32)
+    for d in range(1, ranks):
+        slot = got_zb.at[d]
+        remote(slot, slot, bz_send.at[d], bz_recv.at[d], at_z(my_z)).wait_recv()
+        total += got_zb[d].astype(jnp.float32)
+    part_xb[...] = total.astype(jnp.bfloat16)
+    for d in around:
+        to = low(my_x + d, ring)
+        go(remote(part_xb.at[to], got_rxb.at[d], bx_send.at[d], bx_recv.at[d], at_x(to)))
     gate = line_sum(0)
     up = line_sum(1)
-    back = line_sum(2) * row_p
+    back = part_xb[my_x].astype(jnp.float32)
+    for d in around:
+        slot = got_rxb.at[d]
+        remote(slot, slot, bx_send.at[d], bx_recv.at[d], at_x(my_x)).wait_recv()
+        back += got_rxb[d].astype(jnp.float32)
+    back *= row_p
     sig = 1.0 / (1.0 + jnp.exp(-gate))
     mine = my_x * ranks + my_r
     grads[mine, 0] = (back * up * sig * (1.0 + gate * (1.0 - sig))).astype(jnp.bfloat16)
     grads[mine, 1] = (back * gate * sig).astype(jnp.bfloat16)
 
-    for d in range(1, ranks):
-        to = z_base + low(my_r + d, ranks)
-        go(remote(grads.at[mine], grads.at[mine], gz_send.at[d], gz_recv.at[d], at_z(to)))
-    for d in range(1, ranks):
-        slot = grads.at[my_x * ranks + low(my_r - d, ranks)]
-        remote(slot, slot, gz_send.at[d], gz_recv.at[d], at_z(my_z)).wait_recv()
-    held = grads.at[pl.ds(my_x * ranks, ranks)]
-    for d in around:
-        go(remote(held, held, gx_send.at[d], gx_recv.at[d], at_x(low(my_x + d, ring))))
+    for j in range(1, ranks):
+        go(remote(grads.at[mine], grads.at[mine], gz_send.at[j], gz_recv.at[j], at_z(z_base + (my_r ^ j))))
+    for j in range(ranks):
+        held = grads.at[my_x * ranks + (my_r ^ j)]
+        if j:
+            remote(held, held, gz_send.at[j], gz_recv.at[j], at_z(my_z)).wait_recv()
+        for d in around:
+            go(remote(held, held, gx_send.at[j, d], gx_recv.at[j, d], at_x(low(my_x + d, ring))))
 
     for d in [0] + around:
         owner = low(my_x - d, ring)
         first = owner * ranks
         if d:
-            slot = grads.at[pl.ds(first, ranks)]
-            remote(slot, slot, gx_send.at[d], gx_recv.at[d], at_x(my_x)).wait_recv()
+            for j in range(ranks):
+                slot = grads.at[first + (my_r ^ j)]
+                remote(slot, slot, gx_send.at[j, d], gx_recv.at[j, d], at_x(my_x)).wait_recv()
         both = grads[pl.ds(first, ranks)]
         result = dot_nt(both[:, 0].reshape(ranks * chunk, hidden), wg[...])
         result += dot_nt(both[:, 1].reshape(ranks * chunk, hidden), wu[...])
@@ -411,14 +449,16 @@
     bf = jnp.bfloat16
     vmem = functools.partial(pltpu.VMEM, dtype=bf)
     dma = pltpu.SemaphoreType.DMA
-    any_spec = pl.BlockSpec(memory_space=pl.ANY)
+    hbm_spec = pl.BlockSpec(memory_space=pltpu.HBM)
     vmem_spec = pl.BlockSpec(memory_space=pltpu.VMEM)
     return pl.pallas_call(
         functools.partial(kernel, sizes),
         out_shape=jax.ShapeDtypeStruct((pieces, width), bf),
-        in_specs=[vmem_spec, vmem_spec, vmem_spec, any_spec, any_spec, any_spec],
+        in_specs=[vmem_spec] + [hbm_spec] * 5,
         out_specs=vmem_spec,
         scratch_shapes=[
+            pltpu.VMEM(routes.shape, routes.dtype),
+            vmem(probs.shape),
             vmem((width, hidden)),
             vmem((width, hidden)),
             vmem((width, hidden)),
@@ -433,10 +473,14 @@
             vmem((ranks, 2, chunk, width)),
             vmem((depth, chunk, width)),
             vmem((depth // 2, 2, chunk, width)),
-            vmem((3, ring, ranks * chunk, hidden)),
-            vmem((3, ring, ranks * chunk, hidden)),
-            vmem((3, ranks, chunk, hidden)),
-            vmem((3, ranks, chunk, hidden)),
+            vmem((2, ring, ranks * chunk, hidden)),
+            vmem((2, ring, ranks * chunk, hidden)),
+            vmem((2, ranks, chunk, hidden)),
+            vmem((2, ranks, chunk, hidden)),
+            vmem((ranks, ring, chunk, hidden)),
+            vmem((ranks, ring, chunk, hidden)),
+            vmem((ring, chunk, hidden)),
+            vmem((ring, chunk, hidden)),
             vmem((depth, 2, chunk, hidden)),
             vmem((depth, chunk, width)),
             vmem((depth, chunk, width)),
@@ -445,6 +489,7 @@
             vmem((groups, pieces, width)),
             vmem((groups, pieces, width)),
             dma((3,)),
+            dma((2,)),
             dma(()),
             dma(()),
             dma((2, groups // 2)),
@@ -455,14 +500,18 @@
             dma((2, ring)),
             dma((2, depth)),
             dma((2, depth)),
-            dma((3, ring)),
-            dma((3, ring)),
-            dma((3, ranks)),
-            dma((3, ranks)),
+            dma((2, ring)),
+            dma((2, ring)),
+            dma((2, ranks)),
+            dma((2, ranks)),
             dma((ranks,)),
             dma((ranks,)),
             dma((ring,)),
             dma((ring,)),
+            dma((ranks,)),
+            dma((ranks,)),
+            dma((ranks, ring)),
+            dma((ranks, ring)),
             dma((depth,)),
             dma((depth,)),
             dma((ring,)),
@@ -471,7 +520,7 @@
             dma((groups,)),
         ],
         compiler_params=pltpu.CompilerParams(
-            collective_id=0, has_side_effects=True, vmem_limit_bytes=40 * 1024 * 1024
+            collective_id=0, has_side_effects=True, vmem_limit_bytes=56 * 1024 * 1024
         ),
     )(tokens, routes, probs, w_gate, w_up, w_down)
 

time: 123 us -> 120 us (0.976)
  local copies, waits for them, and re-layouts: 5.18 us -> 1.61 us
    unnamed x12 -> x2, local copies, waits for them, and re-layouts: 4.29 us -> 0.01 us
where the time goes in v3:
time: 120 us
  Pallas kernels  117 us (98%)
  local copies, waits for them, and re-layouts  1.61 us (1%)
  other arithmetic  1.53 us (1%)
    pallas_call x1, Pallas kernels, run(): pl.pallas_call(functools.partial(kernel, sizes), out_shape=jax.ShapeDtype...  117 us

profile of v3, /device:TPU:1, one launch (start us, length us, event | category | flops | bytes accessed | tf_op | source)
XLA Modules:
  0.0 119.8 jit_solution(2813784265853130034)
XLA Ops:
  0.0 0.0 copy-start
  0.0 0.8 reduce
  0.8 0.1 stack_reshape.6
  0.9 0.0 copy-done
  0.9 0.1 reduce.1
  1.0 0.1 stack_reshape.7
  1.1 0.6 pad_maximum_fusion.tok_ref
  1.7 116.6 %shard_map.73 = bf16[16,448]{1,0:T(8,128)(2,1)} custom-call(bf16[2,16,448]{2,1,0:T(8,128)(2,1)} %pad_maximum_fusion.tok_ref, s32[16,8,64]{2,1,0:T(8,128)} %bitcast.14, bf16[16,8,64]{2,1,0:T(8,128)(2,1)} %bitcast.15, bf16[448,1024]{1,0:T(8,128)(2,1)} %bitcast.11, bf16[448,1024]{1,0:T(8,128)(2,1)} %bitcast.12, bf16[448,1024]{1,0:T(8,128)(2,1)} %bitcast.13), custom_call_target="tpu_custom_call" | custom-call | tf_op jit(solution)/shard_map/pallas_call | solution.py:454
  118.4 1.4 %reshape.3 = bf16[1,1,1,7168]{3,2,1,0:T(2,128)(2,1)} reshape(bf16[16,448]{1,0:T(8,128)(2,1)} %shard_map.73) | data formatting | bytes 28672 | tf_op jit(solution)/shard_map/reshape | solution.py:534
Async XLA Ops:
  0.0 0.9 copy-start

commit v4 on v3

--- a/solution.py
+++ b/solution.py
@@ -112,7 +112,7 @@
     lines = groups // 2
     half = depth // 2
     width = tok_ref.shape[2]
-    hidden = wg.shape[1]
+    hidden = wg.shape[1] // 2
     my_g = lax.axis_index("group")
     my_e = lax.axis_index("expert")
     my_x = low(my_e, ring)
@@ -291,30 +291,55 @@
             slot = slot_from(low(my_z - way * d, depth))
             remote(slot, slot, z_send.at[a, d], z_recv.at[a, d], at_z(my_z)).wait_recv()
 
-    def ring_send(q, value):
-        part[q] = value.astype(jnp.bfloat16).reshape(ring, ranks * chunk, hidden)
+    def half_of(weight, h):
+        return weight[:, h * hidden : (h + 1) * hidden]
+
+    def ring_send(q, h, value):
+        part[q, h] = value.astype(jnp.bfloat16).reshape(ring, ranks * chunk, hidden)
         for d in around:
             to = low(my_x + d, ring)
-            go(remote(part.at[q, to], got_rx.at[q, d], rx_send.at[q, d], rx_recv.at[q, d], at_x(to)))
-
-    def line_send(q):
-        total = part[q, my_x].astype(jnp.float32)
-        for d in range(1, ring):
-            slot = got_rx.at[q, d]
-            remote(slot, slot, rx_send.at[q, d], rx_recv.at[q, d], at_x(my_x)).wait_recv()
-            total += got_rx[q, d].astype(jnp.float32)
-        part_z[q] = total.astype(jnp.bfloat16).reshape(ranks, chunk, hidden)
+            go(remote(part.at[q, h, to], got_rx.at[q, h, d], rx_send.at[q, h, d], rx_recv.at[q, h, d], at_x(to)))
+
+    def line_send(q, h):
+        total = part[q, h, my_x].astype(jnp.float32)
+        for d in around:
+            slot = got_rx.at[q, h, d]
+            remote(slot, slot, rx_send.at[q, h, d], rx_recv.at[q, h, d], at_x(my_x)).wait_recv()
+            total += got_rx[q, h, d].astype(jnp.float32)
+        part_z[q, h] = total.astype(jnp.bfloat16).reshape(ranks, chunk, hidden)
         for d in range(1, ranks):
-            to = low(my_r + d, ranks)
-            go(remote(part_z.at[q, to], got_rz.at[q, d], rz_send.at[q, d], rz_recv.at[q, d], at_z(z_base + to)))
-
-    def line_sum(q):
-        total = part_z[q, my_r].astype(jnp.float32)
+            to = my_r ^ d
+            device = at_z(z_base + to)
+            go(remote(part_z.at[q, h, to], got_rz.at[q, h, d], rz_send.at[q, h, d], rz_recv.at[q, h, d], device))
+
+    def line_sum(q, h):
+        total = part_z[q, h, my_r].astype(jnp.float32)
         for d in range(1, ranks):
-            slot = got_rz.at[q, d]
-            remote(slot, slot, rz_send.at[q, d], rz_recv.at[q, d], at_z(my_z)).wait_recv()
-            total += got_rz[q, d].astype(jnp.float32)
+            slot = got_rz.at[q, h, d]
+            remote(slot, slot, rz_send.at[q, h, d], rz_recv.at[q, h, d], at_z(my_z)).wait_recv()
+            total += got_rz[q, h, d].astype(jnp.float32)
         return total
+
+    mine = my_x * ranks + my_r
+
+    def activate(h, back):
+        gate = line_sum(0, h)
+        up = line_sum(1, h)
+        back = back() * row_p
+        sig = 1.0 / (1.0 + jnp.exp(-gate))
+        grads[h, mine, 0] = (back * up * sig * (1.0 + gate * (1.0 - sig))).astype(jnp.bfloat16)
+        grads[h, mine, 1] = (back * gate * sig).astype(jnp.bfloat16)
+        held = grads.at[h, mine]
+        for j in range(1, ranks):
+            go(remote(held, held, gz_send.at[h, j], gz_recv.at[h, j], at_z(z_base + (my_r ^ j))))
+        pass_on(h, 0)
+
+    def pass_on(h, j):
+        held = grads.at[h, my_x * ranks + (my_r ^ j)]
+        if j:
+            remote(held, held, gz_send.at[h, j], gz_recv.at[h, j], at_z(my_z)).wait_recv()
+        for d in around:
+            go(remote(held, held, gx_send.at[h, j, d], gx_recv.at[h, j, d], at_x(low(my_x + d, ring))))
 
     spread(0, tok_ref.at[0], got_a)
     go(remote(tok_ref.at[1], pair.at[my_half], p_send, p_recv, at_z(low(my_z + half, depth))))
@@ -345,20 +370,22 @@
     wait_deep(0, all_z, lambda z: rows.at[chunk_of(z)])
     rows_x = rows[...].reshape(depth * chunk, width)
     weight_copies[0].wait()
-    ring_send(0, exact_dot(rows_x, wg[...]))
     weight_copies[1].wait()
-    ring_send(1, exact_dot(rows_x, wu[...]))
+    for h in range(2):
+        ring_send(0, h, exact_dot(rows_x, half_of(wg, h)))
+        ring_send(1, h, exact_dot(rows_x, half_of(wu, h)))
     wait_deep(1, near, lambda z: rows_b.at[low(z, half)])
     weight_copies[2].wait()
-    back_part = exact_dot(rows_b[...].reshape(depth * chunk, width), wd[...])
-    back_part = back_part.astype(jnp.bfloat16).reshape(ring, ranks, chunk, hidden)
+    rows_g = rows_b[...].reshape(depth * chunk, width)
+    back_part = exact_dot(rows_g, half_of(wd, 0)).astype(jnp.bfloat16).reshape(ring, ranks, chunk, hidden)
     for r in range(ranks):
         part_zb[r] = back_part[:, r]
     for d in range(1, ranks):
         to = my_r ^ d
         go(remote(part_zb.at[to], got_zb.at[d], bz_send.at[d], bz_recv.at[d], at_z(z_base + to)))
-    line_send(0)
-    line_send(1)
+    ring_send(2, 1, exact_dot(rows_g, half_of(wd, 1)))
+    line_send(0, 0)
+    line_send(1, 0)
     total = part_zb[my_r].astype(jnp.float32)
     for d in range(1, ranks):
         slot = got_zb.at[d]
@@ -368,38 +395,37 @@
     for d in around:
         to = low(my_x + d, ring)
         go(remote(part_xb.at[to], got_rxb.at[d], bx_send.at[d], bx_recv.at[d], at_x(to)))
-    gate = line_sum(0)
-    up = line_sum(1)
-    back = part_xb[my_x].astype(jnp.float32)
-    for d in around:
-        slot = got_rxb.at[d]
-        remote(slot, slot, bx_send.at[d], bx_recv.at[d], at_x(my_x)).wait_recv()
-        back += got_rxb[d].astype(jnp.float32)
-    back *= row_p
-    sig = 1.0 / (1.0 + jnp.exp(-gate))
-    mine = my_x * ranks + my_r
-    grads[mine, 0] = (back * up * sig * (1.0 + gate * (1.0 - sig))).astype(jnp.bfloat16)
-    grads[mine, 1] = (back * gate * sig).astype(jnp.bfloat16)
-
-    for j in range(1, ranks):
-        go(remote(grads.at[mine], grads.at[mine], gz_send.at[j], gz_recv.at[j], at_z(z_base + (my_r ^ j))))
-    for j in range(ranks):
-        held = grads.at[my_x * ranks + (my_r ^ j)]
-        if j:
-            remote(held, held, gz_send.at[j], gz_recv.at[j], at_z(my_z)).wait_recv()
+    line_send(0, 1)
+    line_send(1, 1)
+    line_send(2, 1)
+
+    def back_first():
+        back = part_xb[my_x].astype(jnp.float32)
         for d in around:
-            go(remote(held, held, gx_send.at[j, d], gx_recv.at[j, d], at_x(low(my_x + d, ring))))
+            slot = got_rxb.at[d]
+            remote(slot, slot, bx_send.at[d], bx_recv.at[d], at_x(my_x)).wait_recv()
+            back += got_rxb[d].astype(jnp.float32)
+        return back
+
+    activate(0, back_first)
+    activate(1, lambda: line_sum(2, 1))
+    for h in range(2):
+        for j in range(1, ranks):
+            pass_on(h, j)
 
     for d in [0] + around:
         owner = low(my_x - d, ring)
         first = owner * ranks
         if d:
-            for j in range(ranks):
-                slot = grads.at[first + (my_r ^ j)]
-                remote(slot, slot, gx_send.at[j, d], gx_recv.at[j, d], at_x(my_x)).wait_recv()
-        both = grads[pl.ds(first, ranks)]
-        result = dot_nt(both[:, 0].reshape(ranks * chunk, hidden), wg[...])
-        result += dot_nt(both[:, 1].reshape(ranks * chunk, hidden), wu[...])
+            for h in range(2):
+                for j in range(ranks):
+                    slot = grads.at[h, first + (my_r ^ j)]
+                    remote(slot, slot, gx_send.at[h, j, d], gx_recv.at[h, j, d], at_x(my_x)).wait_recv()
+        result = jnp.zeros((ranks * chunk, width), jnp.float32)
+        for h in range(2):
+            both = grads[h, pl.ds(first, ranks)]
+            for q, weight in enumerate((wg, wu)):
+                result += dot_nt(both[:, q].reshape(ranks * chunk, hidden), half_of(weight, h))
         ret[pl.ds(first, ranks)] = result.astype(jnp.bfloat16).reshape(ranks, chunk, width)
         for j in range(ranks):
             at = first + j
@@ -446,6 +472,7 @@
     groups, blocks, ranks, ring, slots = sizes
     depth, pieces, chunk = blocks * ranks, ranks * ring, ring * slots
     width, hidden = w_gate.shape
+    part = hidden // 2
     bf = jnp.bfloat16
     vmem = functools.partial(pltpu.VMEM, dtype=bf)
     dma = pltpu.SemaphoreType.DMA
@@ -473,15 +500,15 @@
             vmem((ranks, 2, chunk, width)),
             vmem((depth, chunk, width)),
             vmem((depth // 2, 2, chunk, width)),
-            vmem((2, ring, ranks * chunk, hidden)),
-            vmem((2, ring, ranks * chunk, hidden)),
-            vmem((2, ranks, chunk, hidden)),
-            vmem((2, ranks, chunk, hidden)),
-            vmem((ranks, ring, chunk, hidden)),
-            vmem((ranks, ring, chunk, hidden)),
-            vmem((ring, chunk, hidden)),
-            vmem((ring, chunk, hidden)),
-            vmem((depth, 2, chunk, hidden)),
+            vmem((3, 2, ring, ranks * chunk, part)),
+            vmem((3, 2, ring, ranks * chunk, part)),
+            vmem((3, 2, ranks, chunk, part)),
+            vmem((3, 2, ranks, chunk, part)),
+            vmem((ranks, ring, chunk, part)),
+            vmem((ranks, ring, chunk, part)),
+            vmem((ring, chunk, part)),
+            vmem((ring, chunk, part)),
+            vmem((2, depth, 2, chunk, part)),
             vmem((depth, chunk, width)),
             vmem((depth, chunk, width)),
             vmem((ring, ranks * slots, width)),
@@ -500,18 +527,18 @@
             dma((2, ring)),
             dma((2, depth)),
             dma((2, depth)),
-            dma((2, ring)),
-            dma((2, ring)),
-            dma((2, ranks)),
-            dma((2, ranks)),
+            dma((3, 2, ring)),
+            dma((3, 2, ring)),
+            dma((3, 2, ranks)),
+            dma((3, 2, ranks)),
             dma((ranks,)),
             dma((ranks,)),
             dma((ring,)),
             dma((ring,)),
-            dma((ranks,)),
-            dma((ranks,)),
-            dma((ranks, ring)),
-            dma((ranks, ring)),
+            dma((2, ranks)),
+            dma((2, ranks)),
+            dma((2, ranks, ring)),
+            dma((2, ranks, ring)),
             dma((depth,)),
             dma((depth,)),
             dma((ring,)),
@@ -520,7 +547,7 @@
             dma((groups,)),
         ],
         compiler_params=pltpu.CompilerParams(
-            collective_id=0, has_side_effects=True, vmem_limit_bytes=56 * 1024 * 1024
+            collective_id=0, has_side_effects=True, vmem_limit_bytes=32 * 1024 * 1024
         ),
     )(tokens, routes, probs, w_gate, w_up, w_down)
 

time: 120 us -> 117 us (0.975)
  Pallas kernels: 117 us -> 110 us
  local copies, waits for them, and re-layouts: 1.61 us -> 5.18 us
    pallas_call x1, Pallas kernels: 117 us -> 110 us  [run(): pl.pallas_call(functools.partial(kernel, sizes), out_shape=jax.ShapeDtype...]
    unnamed x2 -> x12, local copies, waits for them, and re-layouts: 0.01 us -> 4.29 us
where the time goes in v4:
time: 117 us
  Pallas kernels  110 us (94%)
  local copies, waits for them, and re-layouts  5.18 us (4%)
    pallas_call x1, Pallas kernels, run(): pl.pallas_call(functools.partial(kernel, sizes), out_shape=jax.ShapeDtype...  110 us
    unnamed x12, local copies, waits for them, and re-layouts  4.29 us

profile of v4, /device:TPU:1, one launch (start us, length us, event | category | flops | bytes accessed | tf_op | source)
XLA Modules:
  0.0 116.5 jit_solution(14341558956975380893)
XLA Ops:
  0.0 0.0 copy-start.5
  0.0 0.8 reduce
  0.8 0.1 stack_reshape.6
  0.9 0.0 copy-done.5
  0.9 0.0 copy-start.3
  1.0 0.1 reduce.1
  1.0 0.1 stack_reshape.7
  1.1 0.0 copy-start.4
  1.1 0.6 copy-done.3
  1.8 0.1 copy-done.4
  1.9 0.0 copy-start
  1.9 1.2 %copy-done = bf16[1,448,1024]{2,1,0:T(8,128)(2,1)S(1)} copy-done((bf16[1,448,1024]{2,1,0:T(8,128)(2,1)S(1)}, bf16[1,448,1024]{2,1,0:T(8,128)(2,1)}, u32[]{:S(2)}) %copy-start) | copy-done | bytes 917528
  3.1 0.0 copy-start.1
  3.1 1.2 %copy-done.1 = bf16[1,448,1024]{2,1,0:T(8,128)(2,1)S(1)} copy-done((bf16[1,448,1024]{2,1,0:T(8,128)(2,1)S(1)}, bf16[1,448,1024]{2,1,0:T(8,128)(2,1)}, u32[]{:S(2)}) %copy-start.1) | copy-done | bytes 917528
  4.3 0.0 copy-start.2
  4.3 1.2 %copy-done.2 = bf16[1,1024,448]{1,2,0:T(8,128)(2,1)S(1)} copy-done((bf16[1,1024,448]{1,2,0:T(8,128)(2,1)S(1)}, bf16[1,1024,448]{1,2,0:T(8,128)(2,1)}, u32[]{:S(2)}) %copy-start.2) | copy-done | bytes 917528
  5.4 110.4 %shard_map.73 = bf16[16,448]{1,0:T(8,128)(2,1)S(1)} custom-call(bf16[2,16,448]{2,1,0:T(8,128)(2,1)S(1)} %pad_maximum_fusion.tok_ref, s32[16,8,64]{2,1,0:T(8,128)S(1)} %bitcast.14, bf16[16,8,64]{2,1,0:T(8,128)(2,1)S(1)} %bitcast.15, bf16[448,1024]{1,0:T(8,128)(2,1)S(1)} %bitcast.11, bf16[448,1024]{1,0:T(8,128)(2,1)S(1)} %bitcast.12, ...), custom_call_target="tpu_custom_call" | custom-call | tf_op jit(solution)/shard_map/pallas_call | solution.py:481
  115.8 0.7 reshape.3
  (1 shorter events, 0.0 us)
Async XLA Ops:
  0.0 0.9 copy-start.5
  0.9 0.8 copy-start.3
  1.1 0.8 copy-start.4
  1.9 1.2 %copy-start = (bf16[1,448,1024]{2,1,0:T(8,128)(2,1)S(1)}, bf16[1,448,1024]{2,1,0:T(8,128)(2,1)}, u32[]{:S(2)}) copy-start(bf16[1,448,1024]{2,1,0:T(8,128)(2,1)} %param.11) | copy-start | bytes 2752516
  3.1 1.2 %copy-start.1 = (bf16[1,448,1024]{2,1,0:T(8,128)(2,1)S(1)}, bf16[1,448,1024]{2,1,0:T(8,128)(2,1)}, u32[]{:S(2)}) copy-start(bf16[1,448,1024]{2,1,0:T(8,128)(2,1)} %param.12) | copy-start | bytes 2752516
  4.3 1.2 %copy-start.2 = (bf16[1,1024,448]{1,2,0:T(8,128)(2,1)S(1)}, bf16[1,1024,448]{1,2,0:T(8,128)(2,1)}, u32[]{:S(2)}) copy-start(bf16[1,1024,448]{1,2,0:T(8,128)(2,1)} %param.13) | copy-start | bytes 2752516

commit v5 on v4

--- a/solution.py
+++ b/solution.py
@@ -48,13 +48,11 @@
     wg,
     wu,
     wd,
+    tok,
+    landed,
     pair,
     got_a,
     got_b,
-    sel,
-    sel_b,
-    got_x,
-    got_xb,
     blk,
     blk_b,
     rows,
@@ -70,8 +68,6 @@
     grads,
     ret,
     got_ret,
-    ret_x,
-    got_retx,
     scat,
     fin,
     w_sem,
@@ -82,8 +78,6 @@
     a_recv,
     c_send,
     c_recv,
-    x_send,
-    x_recv,
     z_send,
     z_recv,
     rx_send,
@@ -100,8 +94,6 @@
     gx_recv,
     tz_send,
     tz_recv,
-    tx_send,
-    tx_recv,
     tg_send,
     tg_recv,
 ):
@@ -138,6 +130,9 @@
     def at_g(g):
         return (g, my_e)
 
+    def at_gx(g, x):
+        return (g, my_z * ring + x)
+
     def remote(src, dst, send, recv, device):
         return pltpu.make_async_remote_copy(
             src_ref=src, dst_ref=dst, send_sem=send, recv_sem=recv, device_id=device, device_id_type=MESH
@@ -164,13 +159,43 @@
         copy.start()
 
     barrier = pltpu.get_barrier_semaphore()
-    for d in range(1, groups):
-        pl.semaphore_signal(barrier, inc=1, device_id=at_g(low(my_g + d, groups)), device_id_type=MESH)
+    column = [(dg, dx) for dg in range(groups) for dx in range(ring) if dg or dx]
+    for dg, dx in column:
+        device = at_gx(low(my_g + dg, groups), low(my_x + dx, ring))
+        pl.semaphore_signal(barrier, inc=1, device_id=device, device_id_type=MESH)
     for d in range(1, depth):
         pl.semaphore_signal(barrier, inc=1, device_id=at_z(low(my_z + d, depth)), device_id_type=MESH)
-    for d in range(1, ring):
-        pl.semaphore_signal(barrier, inc=1, device_id=at_x(low(my_x + d, ring)), device_id_type=MESH)
-
+
+    shape = (pieces, pieces)
+    row = lax.broadcasted_iota(jnp.int32, shape, 0)
+    by_x = onehot(lax.broadcasted_iota(jnp.int32, shape, 1) == low(row, ranks) * ring + high(row, ranks))
+    for a in range(2):
+        tok[a] = exact_dot(by_x, tok_ref[a]).astype(jnp.bfloat16).reshape(ring, ranks, width)
+    pl.semaphore_wait(barrier, groups * ring - 1 + depth - 1)
+
+    steps = [(dy, dx) for dy in range(lines) for dx in range(ring) if dy or dx]
+    steps.sort(key=lambda step: -min(step[0], lines - step[0]) - min(step[1], ring - step[1]))
+
+    def spread(a, source, target):
+        for dy, dx in steps:
+            y, x = low(my_y + dy, lines), low(my_x + dx, ring)
+            device = at_gx(y * 2 + my_core, x)
+            go(remote(source.at[x], target.at[my_core, my_y, my_x], a_send.at[a, dy, dx], a_recv.at[a, dy, dx], device))
+        target[my_core, my_y, my_x] = source[my_x]
+
+    def share(a, target):
+        for dy, dx in steps:
+            slot = target.at[my_core, low(my_y - dy, lines), low(my_x - dx, ring)]
+            remote(slot, slot, a_send.at[a, dy, dx], a_recv.at[a, dy, dx], at_g(my_g)).wait_recv()
+        mine = target.at[my_core]
+        go(remote(mine, mine, c_send.at[a], c_recv.at[a], at_g(my_y * 2 + 1 - my_core)))
+
+    def wait_share(a, target):
+        slot = target.at[1 - my_core]
+        remote(slot, slot, c_send.at[a], c_recv.at[a], at_g(my_g)).wait_recv()
+
+    spread(0, tok.at[0], got_a)
+    go(remote(tok.at[1], landed, p_send, p_recv, at_z(low(my_z + half, depth))))
     slot_rows = ring * ranks * slots
     token_rows = groups * pieces
 
@@ -181,7 +206,6 @@
     in_group = jnp.max(jnp.where(high(route, blocks) == my_g, 1.0, 0.0), axis=1)
     expert = my_g * blocks + high(my_z, ranks)
     weight = jnp.sum(jnp.where(route == expert, prob_ref[...].astype(jnp.float32), 0.0), axis=1)
-    lane = lax.broadcasted_iota(jnp.int32, (1, columns), 1)
     count = jnp.zeros((1, columns), jnp.float32)
     slot_token = [count] * slots
     slot_weight = [count] * slots
@@ -192,15 +216,6 @@
             slot_token[s] += here * (m % 2 * lines + m // 2)
             slot_weight[s] += here * weight[m : m + 1]
         count += named
-
-    def tokens_of(column):
-        return [
-            jnp.sum(jnp.where(lane == column, token, 0.0), axis=1, keepdims=True).astype(jnp.int32)
-            for token in slot_token
-        ]
-
-    my_tokens = tokens_of(my_e)
-    pair_tokens = [tokens_of((h * half + low(my_z, half)) * ring + my_x) for h in range(2)]
     row = lax.broadcasted_iota(jnp.int32, (chunk, columns), 0)
     owned = z_of(my_x * ranks + my_r) * ring
     row_p = jnp.zeros((chunk, columns), jnp.float32)
@@ -209,70 +224,21 @@
     owner = owned + high(row, slots) == lax.broadcasted_iota(jnp.int32, (chunk, columns), 1)
     row_p = jnp.sum(jnp.where(owner, row_p, 0.0), axis=1, keepdims=True)
 
-    def slot_of(index, tokens):
-        s = low(index, slots)
-        token = jnp.broadcast_to(tokens[0], index.shape)
-        for at in range(1, slots):
-            token = jnp.where(s == at, tokens[at], token)
-        rest = high(index, slots)
-        piece = low(rest, ranks) * ring + high(rest, ranks)
-        return token * pieces + piece
-
-    def picking(tokens):
-        shape = (slot_rows, token_rows)
-        return onehot(
-            slot_of(lax.broadcasted_iota(jnp.int32, shape, 0), tokens)
-            == lax.broadcasted_iota(jnp.int32, shape, 1)
-        )
-
-    shape = (token_rows, slot_rows)
-    unpick = onehot(
-        slot_of(lax.broadcasted_iota(jnp.int32, shape, 1), my_tokens)
-        == lax.broadcasted_iota(jnp.int32, shape, 0)
-    )
-    picks = [picking(my_tokens)] + [picking(tokens) for tokens in pair_tokens]
-    shape = (slot_rows, slot_rows)
-    row = lax.broadcasted_iota(jnp.int32, shape, 0)
-    rest = high(row, slots)
-    turned = (low(rest, ring) * ranks + high(rest, ring)) * slots + low(row, slots)
-    turn = onehot(lax.broadcasted_iota(jnp.int32, shape, 1) == turned)
-    shape = (slot_rows, blocks * slot_rows)
-    row = lax.broadcasted_iota(jnp.int32, shape, 0)
-    rest = high(row, slots)
-    turned = (low(rest, ranks) * ring + high(rest, ranks)) * slots + low(row, slots)
-    fold = onehot(low(lax.broadcasted_iota(jnp.int32, shape, 1), slot_rows) == turned)
-
-    pl.semaphore_wait(barrier, groups + depth + ring - 3)
-
-    far_first = sorted(range(1, lines), key=lambda d: -min(d, lines - d))
-
-    def spread(a, source, target):
-        for d in far_first:
-            to = low(my_y + d, lines) * 2 + my_core
-            go(remote(source, target.at[my_core, my_y], a_send.at[a, d], a_recv.at[a, d], at_g(to)))
-        target[my_core, my_y] = source[...]
-
-    def share(a, target):
-        for d in range(1, lines):
-            slot = target.at[my_core, low(my_y - d, lines)]
-            remote(slot, slot, a_send.at[a, d], a_recv.at[a, d], at_g(my_g)).wait_recv()
-        mine = target.at[my_core]
-        go(remote(mine, mine, c_send.at[a], c_recv.at[a], at_g(my_y * 2 + 1 - my_core)))
-
-    def wait_share(a, target):
-        slot = target.at[1 - my_core]
-        remote(slot, slot, c_send.at[a], c_recv.at[a], at_g(my_g)).wait_recv()
-
-    def ring_swap(a, source, target):
-        for d in range(1, ring):
-            to = low(my_x + d, ring)
-            go(remote(source.at[to], target.at[my_x], x_send.at[a, d], x_recv.at[a, d], at_x(to)))
-        target[my_x] = source[my_x]
-
-    def wait_swap(a, target):
-        for d in range(1, ring):
-            slot = target.at[low(my_x - d, ring)]
-            remote(slot, slot, x_send.at[a, d], x_recv.at[a, d], at_x(my_x)).wait_recv()
+    def picking(z):
+        row = lax.broadcasted_iota(jnp.int32, (slot_rows, columns), 0)
+        token = jnp.zeros((slot_rows, columns), jnp.float32)
+        for s in range(slots):
+            token = jnp.where(low(row, slots) == s, slot_token[s], token)
+        at = z * ring + low(high(row, slots), ring)
+        token = jnp.where(lax.broadcasted_iota(jnp.int32, (slot_rows, columns), 1) == at, token, 0.0)
+        token = jnp.sum(token, axis=1, keepdims=True).astype(jnp.int32)
+        row = lax.broadcasted_iota(jnp.int32, (slot_rows, 1), 0)
+        rest = high(row, slots)
+        wanted = (token * ring + low(rest, ring)) * ranks + high(rest, ring)
+        return onehot(wanted == lax.broadcasted_iota(jnp.int32, (slot_rows, token_rows), 1))
+
+    pick = picking(my_z)
+    pick_pair = [picking(h * half + low(my_z, half)) for h in range(2)]
 
     near = list(range(1, depth // 4 + 1)) + list(range(depth - depth // 4 + 1, depth))
     near.sort(key=lambda d: min(d, depth - d))
@@ -341,31 +307,20 @@
         for d in around:
             go(remote(held, held, gx_send.at[h, j, d], gx_recv.at[h, j, d], at_x(low(my_x + d, ring))))
 
-    spread(0, tok_ref.at[0], got_a)
-    go(remote(tok_ref.at[1], pair.at[my_half], p_send, p_recv, at_z(low(my_z + half, depth))))
-    pair[my_half] = tok_ref[1]
     share(0, got_a)
-    slot = pair.at[1 - my_half]
-    remote(slot, slot, p_send, p_recv, at_z(my_z)).wait_recv()
+    remote(landed, landed, p_send, p_recv, at_z(my_z)).wait_recv()
+    pair[:, my_half] = tok[1]
+    pair[:, 1 - my_half] = landed[...]
     spread(1, pair, got_b)
     wait_share(0, got_a)
-    chosen = exact_dot(picks[0], got_a[...].reshape(token_rows, width)).astype(jnp.bfloat16)
-    sel[...] = chosen.reshape(ring, ranks * slots, width)
-    ring_swap(0, sel, got_x)
-    wait_swap(0, got_x)
-    mixed = exact_dot(turn, got_x[...].reshape(slot_rows, width)).astype(jnp.bfloat16)
-    blk[...] = mixed.reshape(ranks, chunk, width)
+    chosen = exact_dot(pick, got_a[...].reshape(token_rows, width)).astype(jnp.bfloat16)
+    blk[...] = chosen.reshape(ranks, chunk, width)
     send_deep(0, all_z, blk, rows.at[chunk_of(my_z)])
     share(1, got_b)
     wait_share(1, got_b)
     for h in range(2):
-        chosen = exact_dot(picks[1 + h], got_b[:, :, h].reshape(token_rows, width)).astype(jnp.bfloat16)
-        sel_b[:, h] = chosen.reshape(ring, ranks * slots, width)
-    ring_swap(1, sel_b, got_xb)
-    wait_swap(1, got_xb)
-    for h in range(2):
-        mixed = exact_dot(turn, got_xb[:, h].reshape(slot_rows, width)).astype(jnp.bfloat16)
-        blk_b[:, h] = mixed.reshape(ranks, chunk, width)
+        chosen = exact_dot(pick_pair[h], got_b[:, :, :, h].reshape(token_rows, width)).astype(jnp.bfloat16)
+        blk_b[:, h] = chosen.reshape(ranks, chunk, width)
     send_deep(1, near, blk_b, rows_b.at[low(my_z, half)])
     wait_deep(0, all_z, lambda z: rows.at[chunk_of(z)])
     rows_x = rows[...].reshape(depth * chunk, width)
@@ -440,26 +395,34 @@
         source = low(my_z - d, depth)
         slot = got_ret.at[source]
         remote(slot, slot, tz_send.at[source], tz_recv.at[source], at_z(my_z)).wait_recv()
-    folded = exact_dot(fold, got_ret[...].reshape(blocks * slot_rows, width)).astype(jnp.bfloat16)
-    ret_x[...] = folded.reshape(ring, ranks * slots, width)
-    for d in range(1, ring):
-        to = low(my_x + d, ring)
-        go(remote(ret_x.at[to], got_retx.at[my_x], tx_send.at[d], tx_recv.at[d], at_x(to)))
-    got_retx[my_x] = ret_x[my_x]
-    for d in range(1, ring):
-        slot = got_retx.at[low(my_x - d, ring)]
-        remote(slot, slot, tx_send.at[d], tx_recv.at[d], at_x(my_x)).wait_recv()
-    spread_rows = exact_dot(unpick, got_retx[...].reshape(slot_rows, width)).astype(jnp.bfloat16)
-    scat[...] = spread_rows.reshape(groups, pieces, width)
-    for d in range(1, groups):
-        to = low(my_g + d, groups)
-        go(remote(scat.at[low(to, 2) * lines + high(to, 2)], fin.at[d], tg_send.at[d], tg_recv.at[d], at_g(to)))
-    total = scat[low(my_g, 2) * lines + high(my_g, 2)].astype(jnp.float32)
-    for d in range(1, groups):
-        slot = fin.at[d]
-        remote(slot, slot, tg_send.at[d], tg_recv.at[d], at_g(my_g)).wait_recv()
-        total += fin[d].astype(jnp.float32)
-    out_ref[...] = total.astype(jnp.bfloat16)
+    folded = got_ret[:ranks].astype(jnp.float32)
+    for block in range(1, blocks):
+        folded += got_ret[block * ranks : (block + 1) * ranks].astype(jnp.float32)
+    folded = folded.astype(jnp.bfloat16).reshape(slot_rows, width)
+    scattered = lax.dot_general(pick, folded, (((0,), (0,)), ((), ())), preferred_element_type=jnp.float32)
+    scat[...] = scattered.astype(jnp.bfloat16).reshape(groups, ring, ranks, width)
+
+    def place(g):
+        return low(g, 2) * lines + high(g, 2)
+
+    def hops(step):
+        dy = step[0] // 2
+        return min(dy, lines - dy) + min(step[1], ring - step[1])
+
+    column.sort(key=lambda step: -hops(step))
+    for dg, dx in column:
+        g, x = low(my_g + dg, groups), low(my_x + dx, ring)
+        go(remote(scat.at[place(g), x], fin.at[my_x, dg], tg_send.at[dg, dx], tg_recv.at[dg, dx], at_gx(g, x)))
+    fin[my_x, 0] = scat[place(my_g), my_x]
+    shape = (pieces, token_rows)
+    row = lax.broadcasted_iota(jnp.int32, shape, 0)
+    col = lax.broadcasted_iota(jnp.int32, shape, 1)
+    same_x = high(high(col, ranks), groups) == low(row, ring)
+    gather = onehot(same_x & (low(col, ranks) == high(row, ring)))
+    for dg, dx in column:
+        slot = fin.at[low(my_x - dx, ring), dg]
+        remote(slot, slot, tg_send.at[dg, dx], tg_recv.at[dg, dx], at_g(my_g)).wait_recv()
+    out_ref[...] = exact_dot(gather, fin[...].reshape(token_rows, width)).astype(jnp.bfloat16)
 
     for copy in sent:
         copy.wait_send()
@@ -489,13 +452,11 @@
             vmem((width, hidden)),
             vmem((width, hidden)),
             vmem((width, hidden)),
-            vmem((2, pieces, width)),
-            vmem((2, groups // 2, pieces, width)),
-            vmem((2, groups // 2, 2, pieces, width)),
-            vmem((ring, ranks * slots, width)),
-            vmem((ring, 2, ranks * slots, width)),
-            vmem((ring, ranks * slots, width)),
-            vmem((ring, 2, ranks * slots, width)),
+            vmem((2, ring, ranks, width)),
+            vmem((ring, ranks, width)),
+            vmem((ring, 2, ranks, width)),
+            vmem((2, groups // 2, ring, ranks, width)),
+            vmem((2, groups // 2, ring, 2, ranks, width)),
             vmem((ranks, chunk, width)),
             vmem((ranks, 2, chunk, width)),
             vmem((depth, chunk, width)),
@@ -511,20 +472,16 @@
             vmem((2, depth, 2, chunk, part)),
             vmem((depth, chunk, width)),
             vmem((depth, chunk, width)),
-            vmem((ring, ranks * slots, width)),
-            vmem((ring, ranks * slots, width)),
-            vmem((groups, pieces, width)),
-            vmem((groups, pieces, width)),
+            vmem((groups, ring, ranks, width)),
+            vmem((ring, groups, ranks, width)),
             dma((3,)),
             dma((2,)),
             dma(()),
             dma(()),
-            dma((2, groups // 2)),
-            dma((2, groups // 2)),
+            dma((2, groups // 2, ring)),
+            dma((2, groups // 2, ring)),
             dma((2,)),
             dma((2,)),
-            dma((2, ring)),
-            dma((2, ring)),
             dma((2, depth)),
             dma((2, depth)),
             dma((3, 2, ring)),
@@ -541,13 +498,11 @@
             dma((2, ranks, ring)),
             dma((depth,)),
             dma((depth,)),
-            dma((ring,)),
-            dma((ring,)),
-            dma((groups,)),
-            dma((groups,)),
+            dma((groups, ring)),
+            dma((groups, ring)),
         ],
         compiler_params=pltpu.CompilerParams(
-            collective_id=0, has_side_effects=True, vmem_limit_bytes=32 * 1024 * 1024
+            collective_id=0, has_side_effects=True, vmem_limit_bytes=55168 * 1024
         ),
     )(tokens, routes, probs, w_gate, w_up, w_down)
 

time: 117 us -> 110 us (0.940)
  local copies, waits for them, and re-layouts: 5.18 us -> 0.9 us
  Pallas kernels: 110 us -> 107 us
    unnamed x12 -> x2, local copies, waits for them, and re-layouts: 4.29 us -> 0.01 us
    pallas_call x1, Pallas kernels: 110 us -> 107 us  [run(): pl.pallas_call(functools.partial(kernel, sizes), out_shape=jax.ShapeDtype...]
where the time goes in v5:
time: 110 us; the launch traced here: 109 us
  Pallas kernels  107 us (97%)
    pallas_call x1, Pallas kernels, run(): pl.pallas_call(functools.partial(kernel, sizes), out_shape=jax.ShapeDtype...  107 us

profile of v5, /device:TPU:1, one launch (start us, length us, event | category | flops | bytes accessed | tf_op | source)
XLA Modules:
  0.0 109.3 jit_solution(12043011678318636311)
XLA Ops:
  0.0 0.0 copy-start
  0.0 0.8 reduce
  0.8 0.1 stack_reshape.6
  0.9 0.0 copy-done
  0.9 0.1 reduce.1
  1.0 0.1 stack_reshape.7
  1.1 107.5 %shard_map.73 = bf16[16,448]{1,0:T(8,128)(2,1)S(1)} custom-call(bf16[2,16,448]{2,1,0:T(8,128)(2,1)S(1)} %pad_maximum_fusion.tok_ref, s32[16,8,64]{2,1,0:T(8,128)} %bitcast.14, bf16[16,8,64]{2,1,0:T(8,128)(2,1)} %bitcast.15, bf16[448,1024]{1,0:T(8,128)(2,1)} %bitcast.11, bf16[448,1024]{1,0:T(8,128)(2,1)} %bitcast.12, bf16[448,1024]{1,0:T(8,128)(2,1)} %bitcast.13), custom_call_target="tpu_custom_call" | custom-call | tf_op jit(solution)/shard_map/pallas_call | solution.py:444
  108.6 0.7 reshape.3
  (1 shorter events, 0.0 us)
Async XLA Ops:
  0.0 0.9 copy-start

commit v6 on v5

--- a/solution.py
+++ b/solution.py
@@ -36,7 +36,8 @@
 
 def kernel(
     sizes,
-    tok_ref,
+    x_hbm,
+    g_hbm,
     route_hbm,
     prob_hbm,
     wg_hbm,
@@ -48,6 +49,7 @@
     wg,
     wu,
     wd,
+    raw,
     tok,
     landed,
     pair,
@@ -72,6 +74,7 @@
     fin,
     w_sem,
     m_sem,
+    t_sem,
     p_send,
     p_recv,
     a_send,
@@ -103,7 +106,7 @@
     chunk = ring * slots
     lines = groups // 2
     half = depth // 2
-    width = tok_ref.shape[2]
+    width = wg.shape[0]
     hidden = wg.shape[1] // 2
     my_g = lax.axis_index("group")
     my_e = lax.axis_index("expert")
@@ -145,6 +148,11 @@
         copy.start()
         sent.append(copy)
 
+    token_copies = [
+        pltpu.make_async_copy(source, raw.at[at], t_sem.at[at]) for at, source in enumerate((x_hbm, g_hbm))
+    ]
+    for copy in token_copies:
+        copy.start()
     map_copies = [
         pltpu.make_async_copy(source, target, m_sem.at[at])
         for at, (source, target) in enumerate(((route_hbm, route_ref), (prob_hbm, prob_ref)))
@@ -166,11 +174,12 @@
     for d in range(1, depth):
         pl.semaphore_signal(barrier, inc=1, device_id=at_z(low(my_z + d, depth)), device_id_type=MESH)
 
-    shape = (pieces, pieces)
-    row = lax.broadcasted_iota(jnp.int32, shape, 0)
-    by_x = onehot(lax.broadcasted_iota(jnp.int32, shape, 1) == low(row, ranks) * ring + high(row, ranks))
     for a in range(2):
-        tok[a] = exact_dot(by_x, tok_ref[a]).astype(jnp.bfloat16).reshape(ring, ranks, width)
+        token_copies[a].wait()
+        line = raw[a].astype(jnp.float32)
+        order = [r * ring + x for x in range(ring) for r in range(ranks)]
+        cut = jnp.concatenate([line[:, p * width : (p + 1) * width] for p in order], axis=0)
+        tok[a] = cut.astype(jnp.bfloat16).reshape(ring, ranks, width)
     pl.semaphore_wait(barrier, groups * ring - 1 + depth - 1)
 
     steps = [(dy, dx) for dy in range(lines) for dx in range(ring) if dy or dx]
@@ -431,7 +440,7 @@
         remote(ret.at[chunk_of(to)], got_ret.at[my_z], tz_send.at[to], tz_recv.at[my_z], at_z(to)).wait_send()
 
 
-def run(sizes, tokens, routes, probs, w_gate, w_up, w_down):
+def run(sizes, x_row, grad_row, routes, probs, w_gate, w_up, w_down):
     groups, blocks, ranks, ring, slots = sizes
     depth, pieces, chunk = blocks * ranks, ranks * ring, ring * slots
     width, hidden = w_gate.shape
@@ -440,18 +449,18 @@
     vmem = functools.partial(pltpu.VMEM, dtype=bf)
     dma = pltpu.SemaphoreType.DMA
     hbm_spec = pl.BlockSpec(memory_space=pltpu.HBM)
-    vmem_spec = pl.BlockSpec(memory_space=pltpu.VMEM)
     return pl.pallas_call(
         functools.partial(kernel, sizes),
         out_shape=jax.ShapeDtypeStruct((pieces, width), bf),
-        in_specs=[vmem_spec] + [hbm_spec] * 5,
-        out_specs=vmem_spec,
+        in_specs=[hbm_spec] * 7,
+        out_specs=pl.BlockSpec(memory_space=pltpu.VMEM),
         scratch_shapes=[
             pltpu.VMEM(routes.shape, routes.dtype),
             vmem(probs.shape),
             vmem((width, hidden)),
             vmem((width, hidden)),
             vmem((width, hidden)),
+            vmem((2,) + x_row.shape),
             vmem((2, ring, ranks, width)),
             vmem((ring, ranks, width)),
             vmem((ring, 2, ranks, width)),
@@ -475,6 +484,7 @@
             vmem((groups, ring, ranks, width)),
             vmem((ring, groups, ranks, width)),
             dma((3,)),
+            dma((2,)),
             dma((2,)),
             dma(()),
             dma(()),
@@ -502,17 +512,15 @@
             dma((groups, ring)),
         ],
         compiler_params=pltpu.CompilerParams(
-            collective_id=0, has_side_effects=True, vmem_limit_bytes=55168 * 1024
+            collective_id=0, has_side_effects=True, vmem_limit_bytes=55216 * 1024
         ),
-    )(tokens, routes, probs, w_gate, w_up, w_down)
+    )(x_row, grad_row, routes, probs, w_gate, w_up, w_down)
 
 
 def on_device(x_rows, grad_rows, routes, probs, w_gate, w_up, w_down, sizes):
-    groups, blocks, ranks, ring, slots = sizes
-    pieces, width = ranks * ring, w_gate.shape[1]
-    tokens = jnp.stack([x_rows.reshape(pieces, width), grad_rows.reshape(pieces, width)])
+    rows = [array.reshape(1, -1) for array in (x_rows, grad_rows)]
     by_column = [jnp.swapaxes(array[:, :, 0], 1, 2) for array in (routes, probs)]
-    result = run(sizes, tokens, *by_column, w_gate[0], w_up[0], jnp.swapaxes(w_down[0], 0, 1))
+    result = run(sizes, *rows, *by_column, w_gate[0], w_up[0], jnp.swapaxes(w_down[0], 0, 1))
     return result.reshape(x_rows.shape)
 
 

time: 110 us -> 108 us (0.982)
  no operation moved by 1% of the time
where the time goes in v6:
time: 108 us
  Pallas kernels  107 us (99%)
    pallas_call x1, Pallas kernels, run(): pl.pallas_call(functools.partial(kernel, sizes), out_shape=jax.ShapeDtype...  107 us

profile of v6, /device:TPU:1, one launch (start us, length us, event | category | flops | bytes accessed | tf_op | source)
XLA Modules:
  0.0 108.1 jit_solution(5666791584674066068)
XLA Ops:
  0.0 107.4 %shard_map.73 = bf16[16,448]{1,0:T(8,128)(2,1)S(1)} custom-call(bf16[1,7168]{1,0:T(2,128)(2,1)} %bitcast.18, bf16[1,7168]{1,0:T(2,128)(2,1)} %bitcast.19, s32[16,8,64]{2,1,0:T(8,128)} %bitcast.16, bf16[16,8,64]{2,1,0:T(8,128)(2,1)} %bitcast.17, bf16[448,1024]{1,0:T(8,128)(2,1)} %bitcast.13, bf16[448,1024]{1,0:T(8,128)(2,1)} %bitcast.14, ...), custom_call_target="tpu_custom_call" | custom-call | tf_op jit(solution)/shard_map/pallas_call | solution.py:452
  107.4 0.7 reshape.11

commit v7 on v6

--- a/solution.py
+++ b/solution.py
@@ -61,6 +61,7 @@
     rows_b,
     part,
     got_rx,
+    mid,
     part_z,
     got_rz,
     part_zb,
@@ -85,6 +86,8 @@
     z_recv,
     rx_send,
     rx_recv,
+    m_send,
+    m_recv,
     rz_send,
     rz_recv,
     bz_send,
@@ -275,9 +278,40 @@
             to = low(my_x + d, ring)
             go(remote(part.at[q, h, to], got_rx.at[q, h, d], rx_send.at[q, h, d], rx_recv.at[q, h, d], at_x(to)))
 
+    upper, lower = pl.ds(0, ranks * chunk // 2), pl.ds(ranks * chunk // 2, ranks * chunk // 2)
+    right, left, across = low(my_x + 1, ring), low(my_x - 1, ring), low(my_x + 2, ring)
+    legs = ((right, upper, lower), (left, lower, upper))
+
+    def relay_send(q, h, value):
+        part[q, h] = value.astype(jnp.bfloat16).reshape(ring, ranks * chunk, hidden)
+        for at, (to, passed, direct) in enumerate(legs):
+            source = part.at[q, h, across, passed]
+            go(remote(source, mid.at[q, h, at], m_send.at[q, h, at], m_recv.at[q, h, at], at_x(to)))
+        for at, (to, passed, direct) in enumerate(legs):
+            source, target = part.at[q, h, to, direct], got_rx.at[q, h, at, direct]
+            go(remote(source, target, rx_send.at[q, h, at], rx_recv.at[q, h, at], at_x(to)))
+
+    def relay_pass(q, h):
+        for at, (to, passed, direct) in enumerate(legs):
+            slot = mid.at[q, h, at]
+            remote(slot, slot, m_send.at[q, h, at], m_recv.at[q, h, at], at_x(my_x)).wait_recv()
+            total = part[q, h, to, passed].astype(jnp.float32) + mid[q, h, at].astype(jnp.float32)
+            part[q, h, to, passed] = total.astype(jnp.bfloat16)
+            source, target = part.at[q, h, to, passed], got_rx.at[q, h, at, passed]
+            go(remote(source, target, rx_send.at[q, h, 2 + at], rx_recv.at[q, h, 2 + at], at_x(to)))
+
+    def relay_wait(q, h):
+        for at, (to, passed, direct) in enumerate(legs):
+            for sem, rows_at in ((at, direct), (2 + at, passed)):
+                slot = got_rx.at[q, h, at, rows_at]
+                remote(slot, slot, rx_send.at[q, h, sem], rx_recv.at[q, h, sem], at_x(my_x)).wait_recv()
+
     def line_send(q, h):
         total = part[q, h, my_x].astype(jnp.float32)
-        for d in around:
+        if q < 2:
+            relay_wait(q, h)
+            total += got_rx[q, h, 0].astype(jnp.float32) + got_rx[q, h, 1].astype(jnp.float32)
+        for d in around if q == 2 else ():
             slot = got_rx.at[q, h, d]
             remote(slot, slot, rx_send.at[q, h, d], rx_recv.at[q, h, d], at_x(my_x)).wait_recv()
             total += got_rx[q, h, d].astype(jnp.float32)
@@ -336,8 +370,8 @@
     weight_copies[0].wait()
     weight_copies[1].wait()
     for h in range(2):
-        ring_send(0, h, exact_dot(rows_x, half_of(wg, h)))
-        ring_send(1, h, exact_dot(rows_x, half_of(wu, h)))
+        relay_send(0, h, exact_dot(rows_x, half_of(wg, h)))
+        relay_send(1, h, exact_dot(rows_x, half_of(wu, h)))
     wait_deep(1, near, lambda z: rows_b.at[low(z, half)])
     weight_copies[2].wait()
     rows_g = rows_b[...].reshape(depth * chunk, width)
@@ -347,6 +381,9 @@
     for d in range(1, ranks):
         to = my_r ^ d
         go(remote(part_zb.at[to], got_zb.at[d], bz_send.at[d], bz_recv.at[d], at_z(z_base + to)))
+    for h in range(2):
+        for q in range(2):
+            relay_pass(q, h)
     ring_send(2, 1, exact_dot(rows_g, half_of(wd, 1)))
     line_send(0, 0)
     line_send(1, 0)
@@ -472,6 +509,7 @@
             vmem((depth // 2, 2, chunk, width)),
             vmem((3, 2, ring, ranks * chunk, part)),
             vmem((3, 2, ring, ranks * chunk, part)),
+            vmem((2, 2, 2, ranks * chunk // 2, part)),
             vmem((3, 2, ranks, chunk, part)),
             vmem((3, 2, ranks, chunk, part)),
             vmem((ranks, ring, chunk, part)),
@@ -496,6 +534,8 @@
             dma((2, depth)),
             dma((3, 2, ring)),
             dma((3, 2, ring)),
+            dma((2, 2, 2)),
+            dma((2, 2, 2)),
             dma((3, 2, ranks)),
             dma((3, 2, ranks)),
             dma((ranks,)),

time: 108 us -> 108 us (level)
  no operation moved by 1% of the time
where the time goes in v7:
time: 108 us; the launch traced here: 107 us
  Pallas kernels  107 us (99%)
    pallas_call x1, Pallas kernels, run(): pl.pallas_call(functools.partial(kernel, sizes), out_shape=jax.ShapeDtype...  107 us

profile of v7, /device:TPU:1, one launch (start us, length us, event | category | flops | bytes accessed | tf_op | source)
XLA Modules:
  0.0 107.3 jit_solution(15088730124435152239)
XLA Ops:
  0.0 106.6 %shard_map.73 = bf16[16,448]{1,0:T(8,128)(2,1)S(1)} custom-call(bf16[1,7168]{1,0:T(2,128)(2,1)} %bitcast.18, bf16[1,7168]{1,0:T(2,128)(2,1)} %bitcast.19, s32[16,8,64]{2,1,0:T(8,128)} %bitcast.16, bf16[16,8,64]{2,1,0:T(8,128)(2,1)} %bitcast.17, bf16[448,1024]{1,0:T(8,128)(2,1)} %bitcast.13, bf16[448,1024]{1,0:T(8,128)(2,1)} %bitcast.14, ...), custom_call_target="tpu_custom_call" | custom-call | tf_op jit(solution)/shard_map/pallas_call | solution.py:489
  106.6 0.7 reshape.11
